TPU v7x, 32 devices: a whole 2x2x4 slice. The times are simulated.
32 devices in a mesh: section: 4 (over z), rows: 8 (over y, x, core).
Axes of the slice: x: 2, y: 2, z: 4, core: 2. Of those that a mesh axis runs over, the one named last changes fastest.
Arguments:
- latents: bfloat16 [4, 2, 8, 48, 384], P('section', None, 'rows'), may hold values from -6 to 6
- conv_weight: bfloat16 [4, 3, 3, 3, 384, 384], P('section'), may hold values from -0.0625 to 0.0625
- gain: float32 [4, 384], P('section'), may hold values from 0.5 to 2
- bias: float32 [4, 384], P('section'), may hold values from -0.5 to 0.5
Outputs:
- decoded: bfloat16 [4, 2, 8, 48, 384], P('section', None, 'rows')
All inputs are finite; a program needn't handle non-finite values.
Results may differ from a plain program's by a relative error of at most 0.017.
Values may be sent and summed in bfloat16 or wider, within the bound.
A program may use at most 64 MiB of HBM per device.

v0:
```python
import jax
import jax.numpy as jnp
from jax import lax
from jax.sharding import PartitionSpec as P

epsilon = 1e-06


def extended_2(block, sides, width):
    for axis, dim in sides:
        count = lax.axis_size(axis)
        forward = [(i, i + 1) for i in range(count - 1)]
        backward = [(target, source) for source, target in forward]
        low = lax.ppermute(
            lax.slice_in_dim(block, block.shape[dim] - width, None, axis=dim), axis, forward
        )
        high = lax.ppermute(lax.slice_in_dim(block, 0, width, axis=dim), axis, backward)
        block = jnp.concatenate([low, block, high], axis=dim)
    return block


def passed_along(x, axis, by):
    peers = lax.axis_size(axis)
    pairs = [(i, i + by) for i in range(peers) if 0 <= i + by < peers]
    return lax.ppermute(x, axis, pairs)


def normed_silu(values, gain_row):
    widened = values.astype(jnp.float32)
    mean_square = jnp.mean(widened * widened, axis=-1, keepdims=True)
    return jax.nn.silu(widened * lax.rsqrt(mean_square + epsilon) * gain_row).astype(jnp.bfloat16)


def body(latents, conv_weight, gain, bias):
    sections = lax.axis_size("section")
    section_id = lax.axis_index("section")
    frames = latents.shape[1]
    rows_here = latents.shape[2]
    col_count = latents.shape[3]
    channels = latents.shape[4]
    per_block = frames // frames
    item_count = sections * per_block
    step_count = item_count + sections - 1
    kernel = conv_weight[0].reshape(27 * channels, channels)
    gain_row = gain[0]
    bias_row = bias[0]
    pending = latents[0]
    outbox = jnp.zeros_like(pending)
    history = jnp.zeros((2, rows_here, col_count, channels), jnp.bfloat16)
    incoming = jnp.zeros((frames, rows_here, col_count, channels), jnp.bfloat16)

    def advance(step_idx, carry):
        pending, outbox, history, incoming = carry
        slot_index = step_idx % per_block
        fed_item = pending
        current = jnp.where(section_id == 0, fed_item, incoming)
        activated = normed_silu(current, gain_row)
        extended = jnp.concatenate([history, activated], axis=0)
        framed = extended_2(extended, (("rows", 1),), 1)
        padded = jnp.pad(framed, ((0, 0), (0, 0), (1, 1), (0, 0)))
        tap_list = []
        for tap_t in range(3):
            for tap_r in range(3):
                for tap_c in range(3):
                    tap_list.append(
                        padded[
                            tap_t : tap_t + frames,
                            tap_r : tap_r + rows_here,
                            tap_c : tap_c + col_count,
                        ]
                    )
        stacked = jnp.concatenate(tap_list, axis=-1).reshape(
            frames * rows_here * col_count, 27 * channels
        )
        convolved = jnp.dot(stacked, kernel, preferred_element_type=jnp.float32)
        convolved = convolved.reshape(frames, rows_here, col_count, channels)
        result = (current.astype(jnp.float32) + convolved + bias_row).astype(jnp.bfloat16)
        local_item = step_idx - section_id
        is_valid = (local_item >= 0) & (local_item < item_count)
        history = jnp.where(is_valid, extended[-2:], history)
        incoming = passed_along(result, "section", 1)
        shifted_in = passed_along(pending, "section", -1)
        shifted_out = passed_along(outbox, "section", -1)
        pending = jnp.where(slot_index == per_block - 1, shifted_in, pending)
        finished = step_idx - (sections - 1)
        outbox = jnp.where((finished > 0) & (finished % per_block == 0), shifted_out, outbox)
        outbox = jnp.where((section_id == sections - 1) & (finished >= 0), result, outbox)
        return (pending, outbox, history, incoming)

    carry = lax.fori_loop(0, step_count, advance, (pending, outbox, history, incoming))
    return carry[1][None]


def solution(mesh):
    in_specs = (
        P("section", None, "rows", None, None),
        P("section", None, None, None, None, None),
        P("section", None),
        P("section", None),
    )
    out_specs = P("section", None, "rows", None, None)
    return jax.shard_map(body, mesh=mesh, in_specs=in_specs, out_specs=out_specs, check_vma=False)
```

profile of v0, /device:TPU:27, one launch (start us, length us, event | category | flops | bytes accessed | tf_op | source)
XLA Modules:
  0.0 178.2 jit_solution(8427579220715882805)
XLA Ops:
  0.9 176.6 %while.23 = (s32[]{:T(128)}, bf16[2,1,48,384]{3,2,0,1:T(8,128)(2,1)S(1)}, bf16[2,1,48,384]{3,2,0,1:T(8,128)(2,1)S(1)}, bf16[2,1,48,384]{3,2,0,1:T(8,128)(2,1)S(1...) while((s32[]{:T(128)}, ...), condition=%wide.region_2.3_spmd.clone, body=%wide.region_0.2_spmd.clone.sunk | while | flops 768863360 | bytes 18535348 | solution.py:90
  1.9 2.6 %collective-permute-start.2 = (bf16[4,1,48,384]{3,2,0,1:T(8,128)(2,1)S(1)}, bf16[4,1,48,384]{3,2,0,1:T(8,128)(2,1)S(1)}, u32[]{:S(2)}, u32[]{:S(2)}) collective-permute-start(bf16[4,1,48,384]{3,2,0,1:T(8,128)(2,1)S(1)} %pad_maximum_fusion.2), channel_id=1, source_target_pairs={{1,0},{2,1},{3,2},{4,3},{5,4},{6,5},{7,6},{9,8},{10,9},{11,10},{12... | collective-permute-start | bytes 442376 | tf_op jit(solution)/shard_map/while/body/eval_jaxpr/ppermute | solution.py:17
  4.5 3.9 %collective-permute-start.3 = (bf16[4,1,48,384]{3,2,0,1:T(8,128)(2,1)S(1)}, bf16[4,1,48,384]{3,2,0,1:T(8,128)(2,1)S(1)}, u32[]{:S(2)}, u32[]{:S(2)}) collective-permute-start(bf16[4,1,48,384]{3,2,0,1:T(8,128)(2,1)S(1)} %pad_maximum_fusion.2), channel_id=1, source_target_pairs={{0,1},{1,2},{2,3},{3,4},{4,5},{5,6},{6,7},{8,9},{9,10},{10,11},{11... | collective-permute-start | bytes 442376 | tf_op jit(solution)/shard_map/while/body/eval_jaxpr/ppermute | solution.py:14
  14.2 4.8 %select_select_fusion.2 = (bf16[2,1,48,384]{3,2,0,1:T(8,128)(2,1)S(1)}, bf16[2,1,48,384]{3,2,0,1:T(8,128)(2,1)S(1)}) fusion(bf16[2,1,48,384]{3,2,0,1:T(8,128)(2,1)S(1)} %collective-permute-done.1, bf16[2,1,48,384]{3,2,0,1:T(8,128)(2,1)S(1)} %broadcast_select_fusion.8, pred[]{:T(512)S(6)} %gt.13, pred[]{:T(512)S(6)} %and.74, f32[384]{0:T(512)S(1)} %reduce.11, ...), kind=kOutput, calls=%fused_computation.54.clone.1 | convolution fusion | flops 764633088 | bytes 10323458 | tf_op jit(solution)/shard_map/while/body/eval_jaxpr/dot_general | solution.py:75
  20.3 4.9 %collective-permute-done.4 = bf16[2,1,48,384]{3,2,0,1:T(8,128)(2,1)S(1)} collective-permute-done((bf16[2,1,48,384]{3,2,0,1:T(8,128)(2,1)S(1)}, bf16[2,1,48,384]{3,2,0,1:T(8,128)(2,1)S(1)}, u32[]{:S(2)}, u32[]{:S(2)}) %collective-permute-start.4) | collective-permute-done | bytes 73760 | tf_op jit(solution)/shard_map/while/body/eval_jaxpr/ppermute | solution.py:25
  26.2 2.5 %collective-permute-start.2 = (bf16[4,1,48,384]{3,2,0,1:T(8,128)(2,1)S(1)}, bf16[4,1,48,384]{3,2,0,1:T(8,128)(2,1)S(1)}, u32[]{:S(2)}, u32[]{:S(2)}) collective-permute-start(bf16[4,1,48,384]{3,2,0,1:T(8,128)(2,1)S(1)} %pad_maximum_fusion.2), channel_id=1, source_target_pairs={{1,0},{2,1},{3,2},{4,3},{5,4},{6,5},{7,6},{9,8},{10,9},{11,10},{12... | collective-permute-start | bytes 442376 | tf_op jit(solution)/shard_map/while/body/eval_jaxpr/ppermute | solution.py:17
  28.7 4.0 %collective-permute-start.3 = (bf16[4,1,48,384]{3,2,0,1:T(8,128)(2,1)S(1)}, bf16[4,1,48,384]{3,2,0,1:T(8,128)(2,1)S(1)}, u32[]{:S(2)}, u32[]{:S(2)}) collective-permute-start(bf16[4,1,48,384]{3,2,0,1:T(8,128)(2,1)S(1)} %pad_maximum_fusion.2), channel_id=1, source_target_pairs={{0,1},{1,2},{2,3},{3,4},{4,5},{5,6},{6,7},{8,9},{9,10},{10,11},{11... | collective-permute-start | bytes 442376 | tf_op jit(solution)/shard_map/while/body/eval_jaxpr/ppermute | solution.py:14
  32.7 3.2 %collective-permute-start = (bf16[2,1,48,384]{3,2,0,1:T(8,128)(2,1)S(1)}, bf16[2,1,48,384]{3,2,0,1:T(8,128)(2,1)S(1)}, u32[]{:S(2)}, u32[]{:S(2)}) collective-permute-start(bf16[2,1,48,384]{3,2,0,1:T(8,128)(2,1)S(1)} %copy.37), channel_id=1, source_target_pairs={{8,0},{16,8},{24,16},{9,1},{17,9},{25,17},{10,2},{18,10},{26,18},{... | collective-permute-start | bytes 221192 | tf_op jit(solution)/shard_map/while/body/eval_jaxpr/ppermute | solution.py:25
  39.6 4.8 %select_select_fusion.2 = (bf16[2,1,48,384]{3,2,0,1:T(8,128)(2,1)S(1)}, bf16[2,1,48,384]{3,2,0,1:T(8,128)(2,1)S(1)}) fusion(bf16[2,1,48,384]{3,2,0,1:T(8,128)(2,1)S(1)} %collective-permute-done.1, bf16[2,1,48,384]{3,2,0,1:T(8,128)(2,1)S(1)} %broadcast_select_fusion.8, pred[]{:T(512)S(6)} %gt.13, pred[]{:T(512)S(6)} %and.74, f32[384]{0:T(512)S(1)} %reduce.11, ...), kind=kOutput, calls=%fused_computation.54.clone.1 | convolution fusion | flops 764633088 | bytes 10323458 | tf_op jit(solution)/shard_map/while/body/eval_jaxpr/dot_general | solution.py:75
  45.7 4.8 %collective-permute-done.4 = bf16[2,1,48,384]{3,2,0,1:T(8,128)(2,1)S(1)} collective-permute-done((bf16[2,1,48,384]{3,2,0,1:T(8,128)(2,1)S(1)}, bf16[2,1,48,384]{3,2,0,1:T(8,128)(2,1)S(1)}, u32[]{:S(2)}, u32[]{:S(2)}) %collective-permute-start.4) | collective-permute-done | bytes 73760 | tf_op jit(solution)/shard_map/while/body/eval_jaxpr/ppermute | solution.py:25
  51.5 2.6 %collective-permute-start.2 = (bf16[4,1,48,384]{3,2,0,1:T(8,128)(2,1)S(1)}, bf16[4,1,48,384]{3,2,0,1:T(8,128)(2,1)S(1)}, u32[]{:S(2)}, u32[]{:S(2)}) collective-permute-start(bf16[4,1,48,384]{3,2,0,1:T(8,128)(2,1)S(1)} %pad_maximum_fusion.2), channel_id=1, source_target_pairs={{1,0},{2,1},{3,2},{4,3},{5,4},{6,5},{7,6},{9,8},{10,9},{11,10},{12... | collective-permute-start | bytes 442376 | tf_op jit(solution)/shard_map/while/body/eval_jaxpr/ppermute | solution.py:17
  54.2 3.8 %collective-permute-start.3 = (bf16[4,1,48,384]{3,2,0,1:T(8,128)(2,1)S(1)}, bf16[4,1,48,384]{3,2,0,1:T(8,128)(2,1)S(1)}, u32[]{:S(2)}, u32[]{:S(2)}) collective-permute-start(bf16[4,1,48,384]{3,2,0,1:T(8,128)(2,1)S(1)} %pad_maximum_fusion.2), channel_id=1, source_target_pairs={{0,1},{1,2},{2,3},{3,4},{4,5},{5,6},{6,7},{8,9},{9,10},{10,11},{11... | collective-permute-start | bytes 442376 | tf_op jit(solution)/shard_map/while/body/eval_jaxpr/ppermute | solution.py:14
  58.0 3.1 %collective-permute-start = (bf16[2,1,48,384]{3,2,0,1:T(8,128)(2,1)S(1)}, bf16[2,1,48,384]{3,2,0,1:T(8,128)(2,1)S(1)}, u32[]{:S(2)}, u32[]{:S(2)}) collective-permute-start(bf16[2,1,48,384]{3,2,0,1:T(8,128)(2,1)S(1)} %copy.37), channel_id=1, source_target_pairs={{8,0},{16,8},{24,16},{9,1},{17,9},{25,17},{10,2},{18,10},{26,18},{... | collective-permute-start | bytes 221192 | tf_op jit(solution)/shard_map/while/body/eval_jaxpr/ppermute | solution.py:25
  64.8 4.8 %select_select_fusion.2 = (bf16[2,1,48,384]{3,2,0,1:T(8,128)(2,1)S(1)}, bf16[2,1,48,384]{3,2,0,1:T(8,128)(2,1)S(1)}) fusion(bf16[2,1,48,384]{3,2,0,1:T(8,128)(2,1)S(1)} %collective-permute-done.1, bf16[2,1,48,384]{3,2,0,1:T(8,128)(2,1)S(1)} %broadcast_select_fusion.8, pred[]{:T(512)S(6)} %gt.13, pred[]{:T(512)S(6)} %and.74, f32[384]{0:T(512)S(1)} %reduce.11, ...), kind=kOutput, calls=%fused_computation.54.clone.1 | convolution fusion | flops 764633088 | bytes 10323458 | tf_op jit(solution)/shard_map/while/body/eval_jaxpr/dot_general | solution.py:75
  70.9 4.9 %collective-permute-done.4 = bf16[2,1,48,384]{3,2,0,1:T(8,128)(2,1)S(1)} collective-permute-done((bf16[2,1,48,384]{3,2,0,1:T(8,128)(2,1)S(1)}, bf16[2,1,48,384]{3,2,0,1:T(8,128)(2,1)S(1)}, u32[]{:S(2)}, u32[]{:S(2)}) %collective-permute-start.4) | collective-permute-done | bytes 73760 | tf_op jit(solution)/shard_map/while/body/eval_jaxpr/ppermute | solution.py:25
  76.8 2.5 %collective-permute-start.2 = (bf16[4,1,48,384]{3,2,0,1:T(8,128)(2,1)S(1)}, bf16[4,1,48,384]{3,2,0,1:T(8,128)(2,1)S(1)}, u32[]{:S(2)}, u32[]{:S(2)}) collective-permute-start(bf16[4,1,48,384]{3,2,0,1:T(8,128)(2,1)S(1)} %pad_maximum_fusion.2), channel_id=1, source_target_pairs={{1,0},{2,1},{3,2},{4,3},{5,4},{6,5},{7,6},{9,8},{10,9},{11,10},{12... | collective-permute-start | bytes 442376 | tf_op jit(solution)/shard_map/while/body/eval_jaxpr/ppermute | solution.py:17
  79.3 4.0 %collective-permute-start.3 = (bf16[4,1,48,384]{3,2,0,1:T(8,128)(2,1)S(1)}, bf16[4,1,48,384]{3,2,0,1:T(8,128)(2,1)S(1)}, u32[]{:S(2)}, u32[]{:S(2)}) collective-permute-start(bf16[4,1,48,384]{3,2,0,1:T(8,128)(2,1)S(1)} %pad_maximum_fusion.2), channel_id=1, source_target_pairs={{0,1},{1,2},{2,3},{3,4},{4,5},{5,6},{6,7},{8,9},{9,10},{10,11},{11... | collective-permute-start | bytes 442376 | tf_op jit(solution)/shard_map/while/body/eval_jaxpr/ppermute | solution.py:14
  83.3 3.2 %collective-permute-start = (bf16[2,1,48,384]{3,2,0,1:T(8,128)(2,1)S(1)}, bf16[2,1,48,384]{3,2,0,1:T(8,128)(2,1)S(1)}, u32[]{:S(2)}, u32[]{:S(2)}) collective-permute-start(bf16[2,1,48,384]{3,2,0,1:T(8,128)(2,1)S(1)} %copy.37), channel_id=1, source_target_pairs={{8,0},{16,8},{24,16},{9,1},{17,9},{25,17},{10,2},{18,10},{26,18},{... | collective-permute-start | bytes 221192 | tf_op jit(solution)/shard_map/while/body/eval_jaxpr/ppermute | solution.py:25
  90.2 4.8 %select_select_fusion.2 = (bf16[2,1,48,384]{3,2,0,1:T(8,128)(2,1)S(1)}, bf16[2,1,48,384]{3,2,0,1:T(8,128)(2,1)S(1)}) fusion(bf16[2,1,48,384]{3,2,0,1:T(8,128)(2,1)S(1)} %collective-permute-done.1, bf16[2,1,48,384]{3,2,0,1:T(8,128)(2,1)S(1)} %broadcast_select_fusion.8, pred[]{:T(512)S(6)} %gt.13, pred[]{:T(512)S(6)} %and.74, f32[384]{0:T(512)S(1)} %reduce.11, ...), kind=kOutput, calls=%fused_computation.54.clone.1 | convolution fusion | flops 764633088 | bytes 10323458 | tf_op jit(solution)/shard_map/while/body/eval_jaxpr/dot_general | solution.py:75
  96.3 5.0 %collective-permute-done.4 = bf16[2,1,48,384]{3,2,0,1:T(8,128)(2,1)S(1)} collective-permute-done((bf16[2,1,48,384]{3,2,0,1:T(8,128)(2,1)S(1)}, bf16[2,1,48,384]{3,2,0,1:T(8,128)(2,1)S(1)}, u32[]{:S(2)}, u32[]{:S(2)}) %collective-permute-start.4) | collective-permute-done | bytes 73760 | tf_op jit(solution)/shard_map/while/body/eval_jaxpr/ppermute | solution.py:25
  104.6 4.2 %collective-permute-start.3 = (bf16[4,1,48,384]{3,2,0,1:T(8,128)(2,1)S(1)}, bf16[4,1,48,384]{3,2,0,1:T(8,128)(2,1)S(1)}, u32[]{:S(2)}, u32[]{:S(2)}) collective-permute-start(bf16[4,1,48,384]{3,2,0,1:T(8,128)(2,1)S(1)} %pad_maximum_fusion.2), channel_id=1, source_target_pairs={{0,1},{1,2},{2,3},{3,4},{4,5},{5,6},{6,7},{8,9},{9,10},{10,11},{11... | collective-permute-start | bytes 442376 | tf_op jit(solution)/shard_map/while/body/eval_jaxpr/ppermute | solution.py:14
  108.8 3.1 %collective-permute-start = (bf16[2,1,48,384]{3,2,0,1:T(8,128)(2,1)S(1)}, bf16[2,1,48,384]{3,2,0,1:T(8,128)(2,1)S(1)}, u32[]{:S(2)}, u32[]{:S(2)}) collective-permute-start(bf16[2,1,48,384]{3,2,0,1:T(8,128)(2,1)S(1)} %copy.37), channel_id=1, source_target_pairs={{8,0},{16,8},{24,16},{9,1},{17,9},{25,17},{10,2},{18,10},{26,18},{... | collective-permute-start | bytes 221192 | tf_op jit(solution)/shard_map/while/body/eval_jaxpr/ppermute | solution.py:25
  115.7 4.8 %select_select_fusion.2 = (bf16[2,1,48,384]{3,2,0,1:T(8,128)(2,1)S(1)}, bf16[2,1,48,384]{3,2,0,1:T(8,128)(2,1)S(1)}) fusion(bf16[2,1,48,384]{3,2,0,1:T(8,128)(2,1)S(1)} %collective-permute-done.1, bf16[2,1,48,384]{3,2,0,1:T(8,128)(2,1)S(1)} %broadcast_select_fusion.8, pred[]{:T(512)S(6)} %gt.13, pred[]{:T(512)S(6)} %and.74, f32[384]{0:T(512)S(1)} %reduce.11, ...), kind=kOutput, calls=%fused_computation.54.clone.1 | convolution fusion | flops 764633088 | bytes 10323458 | tf_op jit(solution)/shard_map/while/body/eval_jaxpr/dot_general | solution.py:75
  121.8 4.7 %collective-permute-done.4 = bf16[2,1,48,384]{3,2,0,1:T(8,128)(2,1)S(1)} collective-permute-done((bf16[2,1,48,384]{3,2,0,1:T(8,128)(2,1)S(1)}, bf16[2,1,48,384]{3,2,0,1:T(8,128)(2,1)S(1)}, u32[]{:S(2)}, u32[]{:S(2)}) %collective-permute-start.4) | collective-permute-done | bytes 73760 | tf_op jit(solution)/shard_map/while/body/eval_jaxpr/ppermute | solution.py:25
  129.9 4.2 %collective-permute-start.3 = (bf16[4,1,48,384]{3,2,0,1:T(8,128)(2,1)S(1)}, bf16[4,1,48,384]{3,2,0,1:T(8,128)(2,1)S(1)}, u32[]{:S(2)}, u32[]{:S(2)}) collective-permute-start(bf16[4,1,48,384]{3,2,0,1:T(8,128)(2,1)S(1)} %pad_maximum_fusion.2), channel_id=1, source_target_pairs={{0,1},{1,2},{2,3},{3,4},{4,5},{5,6},{6,7},{8,9},{9,10},{10,11},{11... | collective-permute-start | bytes 442376 | tf_op jit(solution)/shard_map/while/body/eval_jaxpr/ppermute | solution.py:14
  134.1 3.5 %collective-permute-start = (bf16[2,1,48,384]{3,2,0,1:T(8,128)(2,1)S(1)}, bf16[2,1,48,384]{3,2,0,1:T(8,128)(2,1)S(1)}, u32[]{:S(2)}, u32[]{:S(2)}) collective-permute-start(bf16[2,1,48,384]{3,2,0,1:T(8,128)(2,1)S(1)} %copy.37), channel_id=1, source_target_pairs={{8,0},{16,8},{24,16},{9,1},{17,9},{25,17},{10,2},{18,10},{26,18},{... | collective-permute-start | bytes 221192 | tf_op jit(solution)/shard_map/while/body/eval_jaxpr/ppermute | solution.py:25
  141.2 4.8 %select_select_fusion.2 = (bf16[2,1,48,384]{3,2,0,1:T(8,128)(2,1)S(1)}, bf16[2,1,48,384]{3,2,0,1:T(8,128)(2,1)S(1)}) fusion(bf16[2,1,48,384]{3,2,0,1:T(8,128)(2,1)S(1)} %collective-permute-done.1, bf16[2,1,48,384]{3,2,0,1:T(8,128)(2,1)S(1)} %broadcast_select_fusion.8, pred[]{:T(512)S(6)} %gt.13, pred[]{:T(512)S(6)} %and.74, f32[384]{0:T(512)S(1)} %reduce.11, ...), kind=kOutput, calls=%fused_computation.54.clone.1 | convolution fusion | flops 764633088 | bytes 10323458 | tf_op jit(solution)/shard_map/while/body/eval_jaxpr/dot_general | solution.py:75
  147.3 4.7 %collective-permute-done.4 = bf16[2,1,48,384]{3,2,0,1:T(8,128)(2,1)S(1)} collective-permute-done((bf16[2,1,48,384]{3,2,0,1:T(8,128)(2,1)S(1)}, bf16[2,1,48,384]{3,2,0,1:T(8,128)(2,1)S(1)}, u32[]{:S(2)}, u32[]{:S(2)}) %collective-permute-start.4) | collective-permute-done | bytes 73760 | tf_op jit(solution)/shard_map/while/body/eval_jaxpr/ppermute | solution.py:25
  155.4 4.2 %collective-permute-start.3 = (bf16[4,1,48,384]{3,2,0,1:T(8,128)(2,1)S(1)}, bf16[4,1,48,384]{3,2,0,1:T(8,128)(2,1)S(1)}, u32[]{:S(2)}, u32[]{:S(2)}) collective-permute-start(bf16[4,1,48,384]{3,2,0,1:T(8,128)(2,1)S(1)} %pad_maximum_fusion.2), channel_id=1, source_target_pairs={{0,1},{1,2},{2,3},{3,4},{4,5},{5,6},{6,7},{8,9},{9,10},{10,11},{11... | collective-permute-start | bytes 442376 | tf_op jit(solution)/shard_map/while/body/eval_jaxpr/ppermute | solution.py:14
  159.5 3.5 %collective-permute-start = (bf16[2,1,48,384]{3,2,0,1:T(8,128)(2,1)S(1)}, bf16[2,1,48,384]{3,2,0,1:T(8,128)(2,1)S(1)}, u32[]{:S(2)}, u32[]{:S(2)}) collective-permute-start(bf16[2,1,48,384]{3,2,0,1:T(8,128)(2,1)S(1)} %copy.37), channel_id=1, source_target_pairs={{8,0},{16,8},{24,16},{9,1},{17,9},{25,17},{10,2},{18,10},{26,18},{... | collective-permute-start | bytes 221192 | tf_op jit(solution)/shard_map/while/body/eval_jaxpr/ppermute | solution.py:25
  166.7 4.8 %select_select_fusion.2 = (bf16[2,1,48,384]{3,2,0,1:T(8,128)(2,1)S(1)}, bf16[2,1,48,384]{3,2,0,1:T(8,128)(2,1)S(1)}) fusion(bf16[2,1,48,384]{3,2,0,1:T(8,128)(2,1)S(1)} %collective-permute-done.1, bf16[2,1,48,384]{3,2,0,1:T(8,128)(2,1)S(1)} %broadcast_select_fusion.8, pred[]{:T(512)S(6)} %gt.13, pred[]{:T(512)S(6)} %and.74, f32[384]{0:T(512)S(1)} %reduce.11, ...), kind=kOutput, calls=%fused_computation.54.clone.1 | convolution fusion | flops 764633088 | bytes 10323458 | tf_op jit(solution)/shard_map/while/body/eval_jaxpr/dot_general | solution.py:75
  172.8 4.7 %collective-permute-done.4 = bf16[2,1,48,384]{3,2,0,1:T(8,128)(2,1)S(1)} collective-permute-done((bf16[2,1,48,384]{3,2,0,1:T(8,128)(2,1)S(1)}, bf16[2,1,48,384]{3,2,0,1:T(8,128)(2,1)S(1)}, u32[]{:S(2)}, u32[]{:S(2)}) %collective-permute-start.4) | collective-permute-done | bytes 73760 | tf_op jit(solution)/shard_map/while/body/eval_jaxpr/ppermute | solution.py:25
  (304 shorter events, 51.4 us)
Async XLA Ops:
  1.9 11.4 %collective-permute-start.2 = (bf16[4,1,48,384]{3,2,0,1:T(8,128)(2,1)S(1)}, bf16[4,1,48,384]{3,2,0,1:T(8,128)(2,1)S(1)}, u32[]{:S(2)}, u32[]{:S(2)}) collective-permute-start(bf16[4,1,48,384]{3,2,0,1:T(8,128)(2,1)S(1)} %pad_maximum_fusion.2), channel_id=1, source_target_pairs={{1,0},{2,1},{3,2},{4,3},{5,4},{6,5},{7,6},{9,8},{10,9},{11,10},{12... | collective-permute-start | bytes 442376 | tf_op jit(solution)/shard_map/while/body/eval_jaxpr/ppermute | solution.py:17
  4.5 8.8 %collective-permute-start.3 = (bf16[4,1,48,384]{3,2,0,1:T(8,128)(2,1)S(1)}, bf16[4,1,48,384]{3,2,0,1:T(8,128)(2,1)S(1)}, u32[]{:S(2)}, u32[]{:S(2)}) collective-permute-start(bf16[4,1,48,384]{3,2,0,1:T(8,128)(2,1)S(1)} %pad_maximum_fusion.2), channel_id=1, source_target_pairs={{0,1},{1,2},{2,3},{3,4},{4,5},{5,6},{6,7},{8,9},{9,10},{10,11},{11... | collective-permute-start | bytes 442376 | tf_op jit(solution)/shard_map/while/body/eval_jaxpr/ppermute | solution.py:14
  8.4 11.9 %collective-permute-start = (bf16[2,1,48,384]{3,2,0,1:T(8,128)(2,1)S(1)}, bf16[2,1,48,384]{3,2,0,1:T(8,128)(2,1)S(1)}, u32[]{:S(2)}, u32[]{:S(2)}) collective-permute-start(bf16[2,1,48,384]{3,2,0,1:T(8,128)(2,1)S(1)} %copy.37), channel_id=1, source_target_pairs={{8,0},{16,8},{24,16},{9,1},{17,9},{25,17},{10,2},{18,10},{26,18},{... | collective-permute-start | bytes 221192 | tf_op jit(solution)/shard_map/while/body/eval_jaxpr/ppermute | solution.py:25
  10.5 3.7 %collective-permute-start.1 = (bf16[2,1,48,384]{3,2,0,1:T(8,128)(2,1)S(1)}, bf16[2,1,48,384]{3,2,0,1:T(8,128)(2,1)S(1)}, u32[]{:S(2)}, u32[]{:S(2)}) collective-permute-start(bf16[2,1,48,384]{3,2,0,1:T(8,128)(2,1)S(1)} %broadcast_select_fusion.8), channel_id=1, source_target_pairs={{8,0},{16,8},{24,16},{9,1},{17,9},{25,17},{10,2},{18,10},{26,18},{... | collective-permute-start | bytes 221192 | tf_op jit(solution)/shard_map/while/body/eval_jaxpr/ppermute | solution.py:25
  19.0 6.2 %collective-permute-start.4 = (bf16[2,1,48,384]{3,2,0,1:T(8,128)(2,1)S(1)}, bf16[2,1,48,384]{3,2,0,1:T(8,128)(2,1)S(1)}, u32[]{:S(2)}, u32[]{:S(2)}) collective-permute-start(bf16[2,1,48,384]{3,2,0,1:T(8,128)(2,1)S(1)} %get-tuple-element.416), channel_id=1, source_target_pairs={{0,8},{8,16},{16,24},{1,9},{9,17},{17,25},{2,10},{10,18},{18,26},{... | collective-permute-start | bytes 221192 | tf_op jit(solution)/shard_map/while/body/eval_jaxpr/ppermute | solution.py:25
  26.2 12.5 %collective-permute-start.2 = (bf16[4,1,48,384]{3,2,0,1:T(8,128)(2,1)S(1)}, bf16[4,1,48,384]{3,2,0,1:T(8,128)(2,1)S(1)}, u32[]{:S(2)}, u32[]{:S(2)}) collective-permute-start(bf16[4,1,48,384]{3,2,0,1:T(8,128)(2,1)S(1)} %pad_maximum_fusion.2), channel_id=1, source_target_pairs={{1,0},{2,1},{3,2},{4,3},{5,4},{6,5},{7,6},{9,8},{10,9},{11,10},{12... | collective-permute-start | bytes 442376 | tf_op jit(solution)/shard_map/while/body/eval_jaxpr/ppermute | solution.py:17
  28.7 10.0 %collective-permute-start.3 = (bf16[4,1,48,384]{3,2,0,1:T(8,128)(2,1)S(1)}, bf16[4,1,48,384]{3,2,0,1:T(8,128)(2,1)S(1)}, u32[]{:S(2)}, u32[]{:S(2)}) collective-permute-start(bf16[4,1,48,384]{3,2,0,1:T(8,128)(2,1)S(1)} %pad_maximum_fusion.2), channel_id=1, source_target_pairs={{0,1},{1,2},{2,3},{3,4},{4,5},{5,6},{6,7},{8,9},{9,10},{10,11},{11... | collective-permute-start | bytes 442376 | tf_op jit(solution)/shard_map/while/body/eval_jaxpr/ppermute | solution.py:14
  32.7 13.0 %collective-permute-start = (bf16[2,1,48,384]{3,2,0,1:T(8,128)(2,1)S(1)}, bf16[2,1,48,384]{3,2,0,1:T(8,128)(2,1)S(1)}, u32[]{:S(2)}, u32[]{:S(2)}) collective-permute-start(bf16[2,1,48,384]{3,2,0,1:T(8,128)(2,1)S(1)} %copy.37), channel_id=1, source_target_pairs={{8,0},{16,8},{24,16},{9,1},{17,9},{25,17},{10,2},{18,10},{26,18},{... | collective-permute-start | bytes 221192 | tf_op jit(solution)/shard_map/while/body/eval_jaxpr/ppermute | solution.py:25
  35.9 3.7 %collective-permute-start.1 = (bf16[2,1,48,384]{3,2,0,1:T(8,128)(2,1)S(1)}, bf16[2,1,48,384]{3,2,0,1:T(8,128)(2,1)S(1)}, u32[]{:S(2)}, u32[]{:S(2)}) collective-permute-start(bf16[2,1,48,384]{3,2,0,1:T(8,128)(2,1)S(1)} %broadcast_select_fusion.8), channel_id=1, source_target_pairs={{8,0},{16,8},{24,16},{9,1},{17,9},{25,17},{10,2},{18,10},{26,18},{... | collective-permute-start | bytes 221192 | tf_op jit(solution)/shard_map/while/body/eval_jaxpr/ppermute | solution.py:25
  44.4 6.2 %collective-permute-start.4 = (bf16[2,1,48,384]{3,2,0,1:T(8,128)(2,1)S(1)}, bf16[2,1,48,384]{3,2,0,1:T(8,128)(2,1)S(1)}, u32[]{:S(2)}, u32[]{:S(2)}) collective-permute-start(bf16[2,1,48,384]{3,2,0,1:T(8,128)(2,1)S(1)} %get-tuple-element.416), channel_id=1, source_target_pairs={{0,8},{8,16},{16,24},{1,9},{9,17},{17,25},{2,10},{10,18},{18,26},{... | collective-permute-start | bytes 221192 | tf_op jit(solution)/shard_map/while/body/eval_jaxpr/ppermute | solution.py:25
  51.5 12.4 %collective-permute-start.2 = (bf16[4,1,48,384]{3,2,0,1:T(8,128)(2,1)S(1)}, bf16[4,1,48,384]{3,2,0,1:T(8,128)(2,1)S(1)}, u32[]{:S(2)}, u32[]{:S(2)}) collective-permute-start(bf16[4,1,48,384]{3,2,0,1:T(8,128)(2,1)S(1)} %pad_maximum_fusion.2), channel_id=1, source_target_pairs={{1,0},{2,1},{3,2},{4,3},{5,4},{6,5},{7,6},{9,8},{10,9},{11,10},{12... | collective-permute-start | bytes 442376 | tf_op jit(solution)/shard_map/while/body/eval_jaxpr/ppermute | solution.py:17
  54.2 9.8 %collective-permute-start.3 = (bf16[4,1,48,384]{3,2,0,1:T(8,128)(2,1)S(1)}, bf16[4,1,48,384]{3,2,0,1:T(8,128)(2,1)S(1)}, u32[]{:S(2)}, u32[]{:S(2)}) collective-permute-start(bf16[4,1,48,384]{3,2,0,1:T(8,128)(2,1)S(1)} %pad_maximum_fusion.2), channel_id=1, source_target_pairs={{0,1},{1,2},{2,3},{3,4},{4,5},{5,6},{6,7},{8,9},{9,10},{10,11},{11... | collective-permute-start | bytes 442376 | tf_op jit(solution)/shard_map/while/body/eval_jaxpr/ppermute | solution.py:14
  58.0 12.9 %collective-permute-start = (bf16[2,1,48,384]{3,2,0,1:T(8,128)(2,1)S(1)}, bf16[2,1,48,384]{3,2,0,1:T(8,128)(2,1)S(1)}, u32[]{:S(2)}, u32[]{:S(2)}) collective-permute-start(bf16[2,1,48,384]{3,2,0,1:T(8,128)(2,1)S(1)} %copy.37), channel_id=1, source_target_pairs={{8,0},{16,8},{24,16},{9,1},{17,9},{25,17},{10,2},{18,10},{26,18},{... | collective-permute-start | bytes 221192 | tf_op jit(solution)/shard_map/while/body/eval_jaxpr/ppermute | solution.py:25
  69.6 6.2 %collective-permute-start.4 = (bf16[2,1,48,384]{3,2,0,1:T(8,128)(2,1)S(1)}, bf16[2,1,48,384]{3,2,0,1:T(8,128)(2,1)S(1)}, u32[]{:S(2)}, u32[]{:S(2)}) collective-permute-start(bf16[2,1,48,384]{3,2,0,1:T(8,128)(2,1)S(1)} %get-tuple-element.416), channel_id=1, source_target_pairs={{0,8},{8,16},{16,24},{1,9},{9,17},{17,25},{2,10},{10,18},{18,26},{... | collective-permute-start | bytes 221192 | tf_op jit(solution)/shard_map/while/body/eval_jaxpr/ppermute | solution.py:25
  76.8 12.5 %collective-permute-start.2 = (bf16[4,1,48,384]{3,2,0,1:T(8,128)(2,1)S(1)}, bf16[4,1,48,384]{3,2,0,1:T(8,128)(2,1)S(1)}, u32[]{:S(2)}, u32[]{:S(2)}) collective-permute-start(bf16[4,1,48,384]{3,2,0,1:T(8,128)(2,1)S(1)} %pad_maximum_fusion.2), channel_id=1, source_target_pairs={{1,0},{2,1},{3,2},{4,3},{5,4},{6,5},{7,6},{9,8},{10,9},{11,10},{12... | collective-permute-start | bytes 442376 | tf_op jit(solution)/shard_map/while/body/eval_jaxpr/ppermute | solution.py:17
  79.3 10.0 %collective-permute-start.3 = (bf16[4,1,48,384]{3,2,0,1:T(8,128)(2,1)S(1)}, bf16[4,1,48,384]{3,2,0,1:T(8,128)(2,1)S(1)}, u32[]{:S(2)}, u32[]{:S(2)}) collective-permute-start(bf16[4,1,48,384]{3,2,0,1:T(8,128)(2,1)S(1)} %pad_maximum_fusion.2), channel_id=1, source_target_pairs={{0,1},{1,2},{2,3},{3,4},{4,5},{5,6},{6,7},{8,9},{9,10},{10,11},{11... | collective-permute-start | bytes 442376 | tf_op jit(solution)/shard_map/while/body/eval_jaxpr/ppermute | solution.py:14
  83.3 13.0 %collective-permute-start = (bf16[2,1,48,384]{3,2,0,1:T(8,128)(2,1)S(1)}, bf16[2,1,48,384]{3,2,0,1:T(8,128)(2,1)S(1)}, u32[]{:S(2)}, u32[]{:S(2)}) collective-permute-start(bf16[2,1,48,384]{3,2,0,1:T(8,128)(2,1)S(1)} %copy.37), channel_id=1, source_target_pairs={{8,0},{16,8},{24,16},{9,1},{17,9},{25,17},{10,2},{18,10},{26,18},{... | collective-permute-start | bytes 221192 | tf_op jit(solution)/shard_map/while/body/eval_jaxpr/ppermute | solution.py:25
  86.5 3.7 %collective-permute-start.1 = (bf16[2,1,48,384]{3,2,0,1:T(8,128)(2,1)S(1)}, bf16[2,1,48,384]{3,2,0,1:T(8,128)(2,1)S(1)}, u32[]{:S(2)}, u32[]{:S(2)}) collective-permute-start(bf16[2,1,48,384]{3,2,0,1:T(8,128)(2,1)S(1)} %broadcast_select_fusion.8), channel_id=1, source_target_pairs={{8,0},{16,8},{24,16},{9,1},{17,9},{25,17},{10,2},{18,10},{26,18},{... | collective-permute-start | bytes 221192 | tf_op jit(solution)/shard_map/while/body/eval_jaxpr/ppermute | solution.py:25
  95.0 6.3 %collective-permute-start.4 = (bf16[2,1,48,384]{3,2,0,1:T(8,128)(2,1)S(1)}, bf16[2,1,48,384]{3,2,0,1:T(8,128)(2,1)S(1)}, u32[]{:S(2)}, u32[]{:S(2)}) collective-permute-start(bf16[2,1,48,384]{3,2,0,1:T(8,128)(2,1)S(1)} %get-tuple-element.416), channel_id=1, source_target_pairs={{0,8},{8,16},{16,24},{1,9},{9,17},{17,25},{2,10},{10,18},{18,26},{... | collective-permute-start | bytes 221192 | tf_op jit(solution)/shard_map/while/body/eval_jaxpr/ppermute | solution.py:25
  102.3 12.5 %collective-permute-start.2 = (bf16[4,1,48,384]{3,2,0,1:T(8,128)(2,1)S(1)}, bf16[4,1,48,384]{3,2,0,1:T(8,128)(2,1)S(1)}, u32[]{:S(2)}, u32[]{:S(2)}) collective-permute-start(bf16[4,1,48,384]{3,2,0,1:T(8,128)(2,1)S(1)} %pad_maximum_fusion.2), channel_id=1, source_target_pairs={{1,0},{2,1},{3,2},{4,3},{5,4},{6,5},{7,6},{9,8},{10,9},{11,10},{12... | collective-permute-start | bytes 442376 | tf_op jit(solution)/shard_map/while/body/eval_jaxpr/ppermute | solution.py:17
  104.6 10.2 %collective-permute-start.3 = (bf16[4,1,48,384]{3,2,0,1:T(8,128)(2,1)S(1)}, bf16[4,1,48,384]{3,2,0,1:T(8,128)(2,1)S(1)}, u32[]{:S(2)}, u32[]{:S(2)}) collective-permute-start(bf16[4,1,48,384]{3,2,0,1:T(8,128)(2,1)S(1)} %pad_maximum_fusion.2), channel_id=1, source_target_pairs={{0,1},{1,2},{2,3},{3,4},{4,5},{5,6},{6,7},{8,9},{9,10},{10,11},{11... | collective-permute-start | bytes 442376 | tf_op jit(solution)/shard_map/while/body/eval_jaxpr/ppermute | solution.py:14
  108.8 13.0 %collective-permute-start = (bf16[2,1,48,384]{3,2,0,1:T(8,128)(2,1)S(1)}, bf16[2,1,48,384]{3,2,0,1:T(8,128)(2,1)S(1)}, u32[]{:S(2)}, u32[]{:S(2)}) collective-permute-start(bf16[2,1,48,384]{3,2,0,1:T(8,128)(2,1)S(1)} %copy.37), channel_id=1, source_target_pairs={{8,0},{16,8},{24,16},{9,1},{17,9},{25,17},{10,2},{18,10},{26,18},{... | collective-permute-start | bytes 221192 | tf_op jit(solution)/shard_map/while/body/eval_jaxpr/ppermute | solution.py:25
  111.9 3.8 %collective-permute-start.1 = (bf16[2,1,48,384]{3,2,0,1:T(8,128)(2,1)S(1)}, bf16[2,1,48,384]{3,2,0,1:T(8,128)(2,1)S(1)}, u32[]{:S(2)}, u32[]{:S(2)}) collective-permute-start(bf16[2,1,48,384]{3,2,0,1:T(8,128)(2,1)S(1)} %broadcast_select_fusion.8), channel_id=1, source_target_pairs={{8,0},{16,8},{24,16},{9,1},{17,9},{25,17},{10,2},{18,10},{26,18},{... | collective-permute-start | bytes 221192 | tf_op jit(solution)/shard_map/while/body/eval_jaxpr/ppermute | solution.py:25
  120.5 6.0 %collective-permute-start.4 = (bf16[2,1,48,384]{3,2,0,1:T(8,128)(2,1)S(1)}, bf16[2,1,48,384]{3,2,0,1:T(8,128)(2,1)S(1)}, u32[]{:S(2)}, u32[]{:S(2)}) collective-permute-start(bf16[2,1,48,384]{3,2,0,1:T(8,128)(2,1)S(1)} %get-tuple-element.416), channel_id=1, source_target_pairs={{0,8},{8,16},{16,24},{1,9},{9,17},{17,25},{2,10},{10,18},{18,26},{... | collective-permute-start | bytes 221192 | tf_op jit(solution)/shard_map/while/body/eval_jaxpr/ppermute | solution.py:25
  127.6 12.7 %collective-permute-start.2 = (bf16[4,1,48,384]{3,2,0,1:T(8,128)(2,1)S(1)}, bf16[4,1,48,384]{3,2,0,1:T(8,128)(2,1)S(1)}, u32[]{:S(2)}, u32[]{:S(2)}) collective-permute-start(bf16[4,1,48,384]{3,2,0,1:T(8,128)(2,1)S(1)} %pad_maximum_fusion.2), channel_id=1, source_target_pairs={{1,0},{2,1},{3,2},{4,3},{5,4},{6,5},{7,6},{9,8},{10,9},{11,10},{12... | collective-permute-start | bytes 442376 | tf_op jit(solution)/shard_map/while/body/eval_jaxpr/ppermute | solution.py:17
  129.9 10.4 %collective-permute-start.3 = (bf16[4,1,48,384]{3,2,0,1:T(8,128)(2,1)S(1)}, bf16[4,1,48,384]{3,2,0,1:T(8,128)(2,1)S(1)}, u32[]{:S(2)}, u32[]{:S(2)}) collective-permute-start(bf16[4,1,48,384]{3,2,0,1:T(8,128)(2,1)S(1)} %pad_maximum_fusion.2), channel_id=1, source_target_pairs={{0,1},{1,2},{2,3},{3,4},{4,5},{5,6},{6,7},{8,9},{9,10},{10,11},{11... | collective-permute-start | bytes 442376 | tf_op jit(solution)/shard_map/while/body/eval_jaxpr/ppermute | solution.py:14
  134.1 13.3 %collective-permute-start = (bf16[2,1,48,384]{3,2,0,1:T(8,128)(2,1)S(1)}, bf16[2,1,48,384]{3,2,0,1:T(8,128)(2,1)S(1)}, u32[]{:S(2)}, u32[]{:S(2)}) collective-permute-start(bf16[2,1,48,384]{3,2,0,1:T(8,128)(2,1)S(1)} %copy.37), channel_id=1, source_target_pairs={{8,0},{16,8},{24,16},{9,1},{17,9},{25,17},{10,2},{18,10},{26,18},{... | collective-permute-start | bytes 221192 | tf_op jit(solution)/shard_map/while/body/eval_jaxpr/ppermute | solution.py:25
  146.0 6.0 %collective-permute-start.4 = (bf16[2,1,48,384]{3,2,0,1:T(8,128)(2,1)S(1)}, bf16[2,1,48,384]{3,2,0,1:T(8,128)(2,1)S(1)}, u32[]{:S(2)}, u32[]{:S(2)}) collective-permute-start(bf16[2,1,48,384]{3,2,0,1:T(8,128)(2,1)S(1)} %get-tuple-element.416), channel_id=1, source_target_pairs={{0,8},{8,16},{16,24},{1,9},{9,17},{17,25},{2,10},{10,18},{18,26},{... | collective-permute-start | bytes 221192 | tf_op jit(solution)/shard_map/while/body/eval_jaxpr/ppermute | solution.py:25
  153.1 12.8 %collective-permute-start.2 = (bf16[4,1,48,384]{3,2,0,1:T(8,128)(2,1)S(1)}, bf16[4,1,48,384]{3,2,0,1:T(8,128)(2,1)S(1)}, u32[]{:S(2)}, u32[]{:S(2)}) collective-permute-start(bf16[4,1,48,384]{3,2,0,1:T(8,128)(2,1)S(1)} %pad_maximum_fusion.2), channel_id=1, source_target_pairs={{1,0},{2,1},{3,2},{4,3},{5,4},{6,5},{7,6},{9,8},{10,9},{11,10},{12... | collective-permute-start | bytes 442376 | tf_op jit(solution)/shard_map/while/body/eval_jaxpr/ppermute | solution.py:17
  155.4 10.5 %collective-permute-start.3 = (bf16[4,1,48,384]{3,2,0,1:T(8,128)(2,1)S(1)}, bf16[4,1,48,384]{3,2,0,1:T(8,128)(2,1)S(1)}, u32[]{:S(2)}, u32[]{:S(2)}) collective-permute-start(bf16[4,1,48,384]{3,2,0,1:T(8,128)(2,1)S(1)} %pad_maximum_fusion.2), channel_id=1, source_target_pairs={{0,1},{1,2},{2,3},{3,4},{4,5},{5,6},{6,7},{8,9},{9,10},{10,11},{11... | collective-permute-start | bytes 442376 | tf_op jit(solution)/shard_map/while/body/eval_jaxpr/ppermute | solution.py:14
  159.5 13.3 %collective-permute-start = (bf16[2,1,48,384]{3,2,0,1:T(8,128)(2,1)S(1)}, bf16[2,1,48,384]{3,2,0,1:T(8,128)(2,1)S(1)}, u32[]{:S(2)}, u32[]{:S(2)}) collective-permute-start(bf16[2,1,48,384]{3,2,0,1:T(8,128)(2,1)S(1)} %copy.37), channel_id=1, source_target_pairs={{8,0},{16,8},{24,16},{9,1},{17,9},{25,17},{10,2},{18,10},{26,18},{... | collective-permute-start | bytes 221192 | tf_op jit(solution)/shard_map/while/body/eval_jaxpr/ppermute | solution.py:25
  171.5 6.0 %collective-permute-start.4 = (bf16[2,1,48,384]{3,2,0,1:T(8,128)(2,1)S(1)}, bf16[2,1,48,384]{3,2,0,1:T(8,128)(2,1)S(1)}, u32[]{:S(2)}, u32[]{:S(2)}) collective-permute-start(bf16[2,1,48,384]{3,2,0,1:T(8,128)(2,1)S(1)} %get-tuple-element.416), channel_id=1, source_target_pairs={{0,8},{8,16},{16,24},{1,9},{9,17},{17,25},{2,10},{10,18},{18,26},{... | collective-permute-start | bytes 221192 | tf_op jit(solution)/shard_map/while/body/eval_jaxpr/ppermute | solution.py:25
  (4 other events, 11.6 us)
where the time goes:
time: 181 us; the launch traced here: 178 us
  starting transfers between devices  90.4 us (50%)
  waiting for transfers between devices  33.8 us (19%)
  matrix products  33.6 us (19%)
  other arithmetic  13.2 us (7%)
  local copies, waits for them, and re-layouts  5.52 us (3%)
    ppermute x21, starting transfers between devices, passed_along(): return lax.ppermute(x, axis, pairs)  45.2 us
    ppermute x21, waiting for transfers between devices, passed_along(): return lax.ppermute(x, axis, pairs)  33.7 us
    dot_general x7, matrix products, advance(): convolved = jnp.dot(stacked, kernel, preferred_element_type=jnp.float32)  33.6 us
    ppermute x7, starting transfers between devices, extended_2(): lax.ppermute(lax.slice_in_dim(block, block.shape[dim] - width, None, axis...  28.1 us
    ppermute x7, starting transfers between devices, extended_2(): lax.ppermute(lax.slice_in_dim(block, 0, width, axis=dim), axis, backward)  17.1 us
    mul x7, other arithmetic, normed_silu(): widened * lax.rsqrt(mean_square + epsilon) * gain_row  4.92 us
    add x7, other arithmetic, advance(): current.astype(jnp.float32) + convolved + bias_row  4.9 us
    while x182, local copies, waits for them, and re-layouts  3.78 us
  transfers between devices with their start and end apart: 35, of which 7 were waited for; matrix products, arithmetic and copies ran while one was open for 25% of the time, Pallas kernels for 0%

commit v1 on v0

v1 whole, which is shorter than its diff:
```python
import functools

import jax
import jax.numpy as jnp
from jax import lax
from jax.experimental import pallas as pl
from jax.experimental.pallas import tpu as pltpu
from jax.sharding import PartitionSpec as P

EPSILON = 1e-06
GROUP = 2


def kernel(
    sections, row_count, group,
    lat_ref, w_hbm, gain_ref, bias_ref, o_ref,
    weights, acts, incoming, outgoing, total,
    w_sem, lat_send, in_recv, out_send, halo_send, halo_recv, own_recv,
):
    frames, cols, ch = lat_ref.shape
    all_frames = sections * frames
    per_block = frames // group
    items = sections * per_block
    rows = group * cols
    section = lax.axis_index("section")
    row = lax.axis_index("rows")
    last = sections - 1

    place = (0, 2, 1)

    def weight_copy(i, j, k):
        return pltpu.make_async_copy(
            w_hbm.at[i, j, k],
            weights.at[i, pl.ds(place[j] * ch, ch), pl.ds(k * ch, ch)],
            w_sem.at[i, j, k],
        )

    for i in (2, 1, 0):
        for j in (1, 0, 2):
            for k in range(3):
                weight_copy(i, j, k).start()

    def weights_here(i):
        for j in (1, 0, 2):
            for k in range(3):
                weight_copy(i, j, k).wait()

    barrier = pltpu.get_barrier_semaphore()
    for peer in range(sections):
        @pl.when(section != peer)
        def _():
            pl.semaphore_signal(barrier, inc=1, device_id={"section": peer})

    @pl.when(row > 0)
    def _():
        pl.semaphore_signal(barrier, inc=1, device_id={"rows": row - 1})

    @pl.when(row < row_count - 1)
    def _():
        pl.semaphore_signal(barrier, inc=1, device_id={"rows": row + 1})

    acts[0:2] = jnp.zeros((2, cols, 3 * ch), jnp.bfloat16)

    @pl.when(row == 0)
    def _():
        acts[:, :, 0:ch] = jnp.zeros((all_frames + 2, cols, ch), jnp.bfloat16)

    @pl.when(row == row_count - 1)
    def _():
        acts[:, :, ch : 2 * ch] = jnp.zeros((all_frames + 2, cols, ch), jnp.bfloat16)

    @pl.when(section == 0)
    def _():
        incoming[0:frames] = lat_ref[...]

    greeted = (
        sections - 1 + jnp.where(row > 0, 1, 0) + jnp.where(row < row_count - 1, 1, 0)
    )
    pl.semaphore_wait(barrier, greeted)

    def lat_copy(part):
        return pltpu.make_async_remote_copy(
            lat_ref.at[pl.ds(part * group, group)],
            incoming.at[pl.ds(section * frames + part * group, group)],
            lat_send.at[part],
            in_recv.at[section * per_block + part],
            device_id={"section": 0},
        )

    @pl.when(section > 0)
    def _():
        for part in range(per_block):
            lat_copy(part).start()

    def pass_copy(item):
        t0 = item * group
        return pltpu.make_async_remote_copy(
            outgoing.at[pl.ds(t0, group)],
            incoming.at[pl.ds(t0, group)],
            out_send.at[item],
            in_recv.at[item],
            device_id={"section": lax.rem(section + 1, sections)},
        )

    def home_copy(item):
        t0 = item * group
        part = lax.rem(item, per_block)
        return pltpu.make_async_remote_copy(
            outgoing.at[pl.ds(t0, group)],
            o_ref.at[pl.ds(part * group, group)],
            out_send.at[item],
            own_recv.at[part],
            device_id={"section": item // per_block},
        )

    def halo_copy(item, side):
        t0 = item * group
        lane = ch if side == 0 else 0
        target = row - 1 if side == 0 else row + 1
        return pltpu.make_async_remote_copy(
            acts.at[pl.ds(t0 + 2, group), :, pl.ds(2 * ch, ch)],
            acts.at[pl.ds(t0 + 2, group), :, pl.ds(lane, ch)],
            halo_send.at[item, side],
            halo_recv.at[item, side],
            device_id={"rows": target},
        )

    def taps(index, count, i, low, high):
        lhs = acts[pl.ds(index, count), :, low:high].reshape(count * cols, high - low)
        return jnp.dot(lhs, weights[i, low:high, :], preferred_element_type=jnp.float32)

    def current_taps(t0, low, high):
        for i in (2, 1, 0):
            h = min(2 - i, group)
            if h < group:
                total[h * cols :, :] += taps(t0 + i + h, group - h, i, low, high)

    gain_row = gain_ref[...]
    bias_row = bias_ref[...]
    col_id = lax.rem(lax.broadcasted_iota(jnp.int32, (rows, ch), 0), cols)

    def step(item, carry):
        t0 = item * group

        @pl.when(item == 0)
        def _():
            total[...] = jnp.zeros((rows, 3 * ch), jnp.float32)

        @pl.when(item > 0)
        def _():
            h = min(2, group)
            total[0 : h * cols, :] = taps(t0, h, 0, 0, 3 * ch)
            if h < group:
                total[h * cols :, :] = jnp.zeros((rows - h * cols, 3 * ch), jnp.float32)
            total[0:cols, :] += taps(t0 + 1, 1, 1, 0, 3 * ch)

        @pl.when((section > 0) | (item >= per_block))
        def _():
            pass_copy(item).wait_recv()

        x = incoming[pl.ds(t0, group)].reshape(rows, ch).astype(jnp.float32)
        mean_square = jnp.mean(x * x, axis=-1, keepdims=True)
        v = x * lax.rsqrt(mean_square + EPSILON) * gain_row
        act = (v * jax.nn.sigmoid(v)).astype(jnp.bfloat16)
        acts[pl.ds(t0 + 2, group), :, 2 * ch : 3 * ch] = act.reshape(group, cols, ch)

        @pl.when(row > 0)
        def _():
            halo_copy(item, 0).start()

        @pl.when(row < row_count - 1)
        def _():
            halo_copy(item, 1).start()

        @pl.when(item == 0)
        def _():
            weights_here(2)
            weights_here(1)

        current_taps(t0, 2 * ch, 3 * ch)

        @pl.when(row < row_count - 1)
        def _():
            halo_copy(item, 0).wait_recv()

        @pl.when(row > 0)
        def _():
            halo_copy(item, 1).wait_recv()

        current_taps(t0, 0, 2 * ch)

        left = pltpu.roll(total[:, 0:ch], 1, 0)
        left = jnp.where(col_id == 0, 0.0, left)
        right = pltpu.roll(total[:, 2 * ch : 3 * ch], rows - 1, 0)
        right = jnp.where(col_id == cols - 1, 0.0, right)
        y = x + (left + total[:, ch : 2 * ch] + right) + bias_row
        y = y.astype(jnp.bfloat16).reshape(group, cols, ch)

        home = (section == last) & (item >= last * per_block)

        @pl.when(home)
        def _():
            o_ref[pl.ds(t0 - last * frames, group)] = y

        @pl.when(jnp.logical_not(home))
        def _():
            outgoing[pl.ds(t0, group)] = y

        @pl.when(section < last)
        def _():
            pass_copy(item).start()

        @pl.when((section == last) & (item < last * per_block))
        def _():
            home_copy(item).start()

        @pl.when(item == 0)
        def _():
            weights_here(0)

        return carry

    lax.fori_loop(0, items, step, 0)

    @pl.when(section > 0)
    def _():
        for part in range(per_block):
            lat_copy(part).wait_send()

    def finish(item, carry):
        @pl.when(row > 0)
        def _():
            halo_copy(item, 0).wait_send()

        @pl.when(row < row_count - 1)
        def _():
            halo_copy(item, 1).wait_send()

        @pl.when((section < last) | (item < last * per_block))
        def _():
            pass_copy(item).wait_send()

        return carry

    lax.fori_loop(0, items, finish, 0)

    @pl.when(section < last)
    def _():
        for part in range(per_block):
            home_copy(part).wait_recv()


def solution(mesh):
    sections = mesh.shape["section"]
    row_count = mesh.shape["rows"]

    def body(latents, conv_weight, gain, bias):
        _, frames, _, cols, ch = latents.shape
        group = GROUP
        all_frames = sections * frames
        per_block = frames // group
        items = sections * per_block
        rows = group * cols
        dma = pltpu.SemaphoreType.DMA
        vmem = pl.BlockSpec(memory_space=pltpu.VMEM)
        out = pl.pallas_call(
            functools.partial(kernel, sections, row_count, group),
            out_shape=jax.ShapeDtypeStruct((frames, cols, ch), jnp.bfloat16),
            in_specs=[vmem, pl.BlockSpec(memory_space=pl.ANY), vmem, vmem],
            out_specs=vmem,
            scratch_shapes=[
                pltpu.VMEM((3, 3 * ch, 3 * ch), jnp.bfloat16),
                pltpu.VMEM((all_frames + 2, cols, 3 * ch), jnp.bfloat16),
                pltpu.VMEM((all_frames, cols, ch), jnp.bfloat16),
                pltpu.VMEM((all_frames, cols, ch), jnp.bfloat16),
                pltpu.VMEM((rows, 3 * ch), jnp.float32),
                dma((3, 3, 3)),
                dma((per_block,)),
                dma((items,)),
                dma((items,)),
                dma((items, 2)),
                dma((items, 2)),
                dma((per_block,)),
            ],
            compiler_params=pltpu.CompilerParams(
                collective_id=0, has_side_effects=True, vmem_limit_bytes=48 * 2**20
            ),
            cost_estimate=pl.CostEstimate(
                flops=2 * all_frames * cols * 27 * ch * ch,
                bytes_accessed=27 * ch * ch * 2,
                transcendentals=all_frames * cols * ch,
            ),
        )(latents.reshape(frames, cols, ch), conv_weight[0], gain, bias)
        return out.reshape(latents.shape)

    in_specs = (
        P("section", None, "rows", None, None),
        P("section", None, None, None, None, None),
        P("section", None),
        P("section", None),
    )
    out_specs = P("section", None, "rows", None, None)
    return jax.shard_map(body, mesh=mesh, in_specs=in_specs, out_specs=out_specs, check_vma=False)
```

time: 181 us -> 49.7 us (0.27); the launches traced: 178 us -> 49.5 us
  starting transfers between devices: 90.4 us -> 0 us
  Pallas kernels: 0 us -> 46.6 us
  waiting for transfers between devices: 33.8 us -> 0 us
  matrix products: 33.6 us -> 0 us
  other arithmetic: 13.2 us -> 0 us
  local copies, waits for them, and re-layouts: 5.52 us -> 2.88 us
    ppermute x35 -> x0, starting transfers between devices: 90.4 us -> none  [the longest x21 45.2 us: passed_along(): return lax.ppermute(x, axis, pairs)]
    pallas_call x0 -> x1, Pallas kernels: none -> 46.6 us  [body(): pl.pallas_call(functools.partial(kernel, sections, row_count, group), out...]
    ppermute x35 -> x0, waiting for transfers between devices: 33.8 us -> none  [the longest x21 33.7 us: passed_along(): return lax.ppermute(x, axis, pairs)]
    dot_general x7 -> x0, matrix products: 33.6 us -> none  [advance(): convolved = jnp.dot(stacked, kernel, preferred_element_type=jnp.float32)]
    mul x7 -> x0, other arithmetic: 4.92 us -> none  [normed_silu(): widened * lax.rsqrt(mean_square + epsilon) * gain_row]
    add x7 -> x0, other arithmetic: 4.9 us -> none  [advance(): current.astype(jnp.float32) + convolved + bias_row]
    while x182 -> x0, local copies, waits for them, and re-layouts: 3.78 us -> none
  transfers between devices with their start and end apart: 35 -> 0, of which waited for: 7 -> 0; matrix products, arithmetic and copies ran while one was open for 25% -> 0% of each run, Pallas kernels for 0% -> 0%
where the time goes in v1:
time: 49.7 us; the launch traced here: 49.5 us
  Pallas kernels  46.6 us (94%)
  local copies, waits for them, and re-layouts  2.88 us (6%)
    pallas_call x1, Pallas kernels, body(): pl.pallas_call(functools.partial(kernel, sections, row_count, group), out...  46.6 us
    unnamed x7, local copies, waits for them, and re-layouts  2.88 us

profile of v1, /device:TPU:27, one launch (start us, length us, event | category | flops | bytes accessed | tf_op | source)
XLA Modules:
  0.0 49.5 jit_solution(8744659509751480549)
XLA Ops:
  0.0 0.0 copy-start
  0.0 0.9 %copy-done = bf16[1,2,1,48,384]{4,3,2,1,0:T(8,128)(2,1)S(1)} copy-done((bf16[1,2,1,48,384]{4,3,2,1,0:T(8,128)(2,1)S(1)}, bf16[1,2,1,48,384]{4,3,2,1,0:T(8,128)(2,1)}, u32[]{:S(2)}) %copy-start) | copy-done | bytes 73752
  0.9 0.0 copy-start.1
  0.9 0.7 %copy-done.1 = f32[1,384]{1,0:T(1,128)S(1)} copy-done((f32[1,384]{1,0:T(1,128)S(1)}, f32[1,384]{1,0:T(1,128)}, u32[]{:S(2)}) %copy-start.1) | copy-done | bytes 1560
  1.6 0.0 copy-start.2
  1.6 0.7 %copy-done.2 = f32[1,384]{1,0:T(1,128)S(1)} copy-done((f32[1,384]{1,0:T(1,128)S(1)}, f32[1,384]{1,0:T(1,128)}, u32[]{:S(2)}) %copy-start.2) | copy-done | bytes 1560
  2.2 46.6 %shard_map.46 = bf16[2,48,384]{2,1,0:T(8,128)(2,1)S(1)} custom-call(bf16[2,48,384]{2,1,0:T(8,128)(2,1)S(1)} %bitcast.6, bf16[3,3,3,384,384]{4,3,2,1,0:T(8,128)(2,1)} %bitcast.7, f32[1,384]{1,0:T(1,128)S(1)} %copy-done.1, f32[1,384]{1,0:T(1,128)S(1)} %copy-done.2), custom_call_target="tpu_custom_call" | custom-call | flops 3057647616 | bytes 7962624 | tf_op jit(solution)/shard_map/pallas_call | solution.py:266
  48.9 0.6 %copy.7 = bf16[1,2,1,48,384]{4,3,2,1,0:T(8,128)(2,1)} copy(bf16[1,2,1,48,384]{4,3,2,1,0:T(8,128)(2,1)S(1)} %bitcast.5) | data formatting | bytes 147456
Async XLA Ops:
  0.0 0.9 %copy-start = (bf16[1,2,1,48,384]{4,3,2,1,0:T(8,128)(2,1)S(1)}, bf16[1,2,1,48,384]{4,3,2,1,0:T(8,128)(2,1)}, u32[]{:S(2)}) copy-start(bf16[1,2,1,48,384]{4,3,2,1,0:T(8,128)(2,1)} %param.4) | copy-start | bytes 221188
  0.9 0.7 %copy-start.1 = (f32[1,384]{1,0:T(1,128)S(1)}, f32[1,384]{1,0:T(1,128)}, u32[]{:S(2)}) copy-start(f32[1,384]{1,0:T(1,128)} %gain_ref.1) | copy-start | bytes 4612
  1.6 0.7 %copy-start.2 = (f32[1,384]{1,0:T(1,128)S(1)}, f32[1,384]{1,0:T(1,128)}, u32[]{:S(2)}) copy-start(f32[1,384]{1,0:T(1,128)} %bias_ref.1) | copy-start | bytes 4612

commit v2 on v1

--- a/solution.py
+++ b/solution.py
@@ -13,9 +13,9 @@
 
 def kernel(
     sections, row_count, group,
-    lat_ref, w_hbm, gain_ref, bias_ref, o_ref,
-    weights, acts, incoming, outgoing, total,
-    w_sem, lat_send, in_recv, out_send, halo_send, halo_recv, own_recv,
+    lat_ref, w_hbm, gain_hbm, bias_hbm, o_ref,
+    weights, acts, incoming, outgoing, total, gain_ref, bias_ref,
+    w_sem, small_sem, lat_send, in_recv, out_send, halo_send, halo_recv, own_recv,
 ):
     frames, cols, ch = lat_ref.shape
     all_frames = sections * frames
@@ -26,24 +26,42 @@
     row = lax.axis_index("rows")
     last = sections - 1
 
-    place = (0, 2, 1)
+    place = {
+        (1, 0): 0, (1, 2): 1, (2, 0): 2, (2, 2): 3,
+        (1, 1): 4, (2, 1): 5,
+        (0, 0): 6, (0, 2): 7, (0, 1): 8,
+    }
+    own_taps = ((1, 1), (2, 1))
+    halo_taps = ((1, 0), (1, 2), (2, 0), (2, 2))
+    old_taps = ((0, 0), (0, 2), (0, 1))
 
     def weight_copy(i, j, k):
         return pltpu.make_async_copy(
             w_hbm.at[i, j, k],
-            weights.at[i, pl.ds(place[j] * ch, ch), pl.ds(k * ch, ch)],
+            weights.at[pl.ds(place[i, j] * ch, ch), pl.ds(k * ch, ch)],
             w_sem.at[i, j, k],
         )
 
-    for i in (2, 1, 0):
-        for j in (1, 0, 2):
-            for k in range(3):
-                weight_copy(i, j, k).start()
-
-    def weights_here(i):
-        for j in (1, 0, 2):
+    def weights_here(taps):
+        for i, j in taps:
             for k in range(3):
                 weight_copy(i, j, k).wait()
+
+    gain_copy = pltpu.make_async_copy(gain_hbm, gain_ref, small_sem.at[0])
+    bias_copy = pltpu.make_async_copy(bias_hbm, bias_ref, small_sem.at[1])
+    first_copy = pltpu.make_async_copy(
+        lat_ref, incoming.at[pl.ds(0, frames)], small_sem.at[2]
+    )
+
+    @pl.when(section == 0)
+    def _():
+        first_copy.start()
+
+    gain_copy.start()
+    bias_copy.start()
+    for i, j in own_taps + halo_taps + old_taps:
+        for k in range(3):
+            weight_copy(i, j, k).start()
 
     barrier = pltpu.get_barrier_semaphore()
     for peer in range(sections):
@@ -68,10 +86,6 @@
     @pl.when(row == row_count - 1)
     def _():
         acts[:, :, ch : 2 * ch] = jnp.zeros((all_frames + 2, cols, ch), jnp.bfloat16)
-
-    @pl.when(section == 0)
-    def _():
-        incoming[0:frames] = lat_ref[...]
 
     greeted = (
         sections - 1 + jnp.where(row > 0, 1, 0) + jnp.where(row < row_count - 1, 1, 0)
@@ -125,34 +139,32 @@
             device_id={"rows": target},
         )
 
-    def taps(index, count, i, low, high):
-        lhs = acts[pl.ds(index, count), :, low:high].reshape(count * cols, high - low)
-        return jnp.dot(lhs, weights[i, low:high, :], preferred_element_type=jnp.float32)
-
-    def current_taps(t0, low, high):
-        for i in (2, 1, 0):
-            h = min(2 - i, group)
-            if h < group:
-                total[h * cols :, :] += taps(t0 + i + h, group - h, i, low, high)
-
+    def product(starts, low, high, top):
+        parts = [
+            acts[pl.ds(start, group), :, low:high].reshape(rows, high - low)
+            for start in starts
+        ]
+        lhs = jnp.concatenate(parts, axis=-1)
+        rhs = weights[top * ch : top * ch + lhs.shape[1], :]
+        return jnp.dot(lhs, rhs, preferred_element_type=jnp.float32)
+
+    gain_copy.wait()
+    bias_copy.wait()
     gain_row = gain_ref[...]
     bias_row = bias_ref[...]
+
+    @pl.when(section == 0)
+    def _():
+        first_copy.wait()
+
     col_id = lax.rem(lax.broadcasted_iota(jnp.int32, (rows, ch), 0), cols)
 
     def step(item, carry):
         t0 = item * group
 
-        @pl.when(item == 0)
-        def _():
-            total[...] = jnp.zeros((rows, 3 * ch), jnp.float32)
-
         @pl.when(item > 0)
         def _():
-            h = min(2, group)
-            total[0 : h * cols, :] = taps(t0, h, 0, 0, 3 * ch)
-            if h < group:
-                total[h * cols :, :] = jnp.zeros((rows - h * cols, 3 * ch), jnp.float32)
-            total[0:cols, :] += taps(t0 + 1, 1, 1, 0, 3 * ch)
+            total[...] = product((t0,), 0, 3 * ch, 6)
 
         @pl.when((section > 0) | (item >= per_block))
         def _():
@@ -174,10 +186,18 @@
 
         @pl.when(item == 0)
         def _():
-            weights_here(2)
-            weights_here(1)
-
-        current_taps(t0, 2 * ch, 3 * ch)
+            weights_here(own_taps)
+
+        own = product((t0 + 1, t0 + 2), 2 * ch, 3 * ch, 4)
+
+        @pl.when(item == 0)
+        def _():
+            total[...] = own
+            weights_here(halo_taps)
+
+        @pl.when(item > 0)
+        def _():
+            total[...] += own
 
         @pl.when(row < row_count - 1)
         def _():
@@ -187,13 +207,12 @@
         def _():
             halo_copy(item, 1).wait_recv()
 
-        current_taps(t0, 0, 2 * ch)
-
-        left = pltpu.roll(total[:, 0:ch], 1, 0)
+        summed = total[...] + product((t0 + 1, t0 + 2), 0, 2 * ch, 0)
+        left = pltpu.roll(summed[:, 0:ch], 1, 0)
         left = jnp.where(col_id == 0, 0.0, left)
-        right = pltpu.roll(total[:, 2 * ch : 3 * ch], rows - 1, 0)
+        right = pltpu.roll(summed[:, 2 * ch : 3 * ch], rows - 1, 0)
         right = jnp.where(col_id == cols - 1, 0.0, right)
-        y = x + (left + total[:, ch : 2 * ch] + right) + bias_row
+        y = x + (left + summed[:, ch : 2 * ch] + right) + bias_row
         y = y.astype(jnp.bfloat16).reshape(group, cols, ch)
 
         home = (section == last) & (item >= last * per_block)
@@ -216,7 +235,7 @@
 
         @pl.when(item == 0)
         def _():
-            weights_here(0)
+            weights_here(old_taps)
 
         return carry
 
@@ -266,15 +285,18 @@
         out = pl.pallas_call(
             functools.partial(kernel, sections, row_count, group),
             out_shape=jax.ShapeDtypeStruct((frames, cols, ch), jnp.bfloat16),
-            in_specs=[vmem, pl.BlockSpec(memory_space=pl.ANY), vmem, vmem],
+            in_specs=[pl.BlockSpec(memory_space=pl.ANY)] * 4,
             out_specs=vmem,
             scratch_shapes=[
-                pltpu.VMEM((3, 3 * ch, 3 * ch), jnp.bfloat16),
+                pltpu.VMEM((9 * ch, 3 * ch), jnp.bfloat16),
                 pltpu.VMEM((all_frames + 2, cols, 3 * ch), jnp.bfloat16),
                 pltpu.VMEM((all_frames, cols, ch), jnp.bfloat16),
                 pltpu.VMEM((all_frames, cols, ch), jnp.bfloat16),
                 pltpu.VMEM((rows, 3 * ch), jnp.float32),
+                pltpu.VMEM((1, ch), jnp.float32),
+                pltpu.VMEM((1, ch), jnp.float32),
                 dma((3, 3, 3)),
+                dma((3,)),
                 dma((per_block,)),
                 dma((items,)),
                 dma((items,)),
@@ -283,7 +305,7 @@
                 dma((per_block,)),
             ],
             compiler_params=pltpu.CompilerParams(
-                collective_id=0, has_side_effects=True, vmem_limit_bytes=48 * 2**20
+                collective_id=0, has_side_effects=True, vmem_limit_bytes=60 * 2**20
             ),
             cost_estimate=pl.CostEstimate(
                 flops=2 * all_frames * cols * 27 * ch * ch,

time: 49.7 us -> 48.6 us (0.978)
  local copies, waits for them, and re-layouts: 2.88 us -> 1.52 us
    unnamed x7 -> x1, local copies, waits for them, and re-layouts: 2.88 us -> 1.52 us
where the time goes in v2:
time: 48.6 us; the launch traced here: 48.5 us
  Pallas kernels  47 us (97%)
  local copies, waits for them, and re-layouts  1.52 us (3%)
    pallas_call x1, Pallas kernels, body(): pl.pallas_call(functools.partial(kernel, sections, row_count, group), out...  47 us
    unnamed x1, local copies, waits for them, and re-layouts  1.52 us

profile of v2, /device:TPU:27, one launch (start us, length us, event | category | flops | bytes accessed | tf_op | source)
XLA Modules:
  0.0 48.5 jit_solution(5735414309906274604)
XLA Ops:
  0.0 47.0 %shard_map.46 = bf16[2,48,384]{2,1,0:T(8,128)(2,1)} custom-call(bf16[2,48,384]{2,1,0:T(8,128)(2,1)} %bitcast.7, bf16[3,3,3,384,384]{4,3,2,1,0:T(8,128)(2,1)} %bitcast.6, f32[1,384]{1,0:T(1,128)} %gain_hbm.1, f32[1,384]{1,0:T(1,128)} %bias_hbm.1), custom_call_target="tpu_custom_call" | custom-call | flops 3057647616 | bytes 7962624 | tf_op jit(solution)/shard_map/pallas_call | solution.py:285
  47.0 1.5 %copy.7 = bf16[1,2,1,48,384]{4,3,2,1,0:T(8,128)(2,1)} copy(bf16[1,2,1,48,384]{4,3,2,1,0:T(8,128)(2,1)} %bitcast.5) | data formatting | bytes 147456

commit v3 on v2

--- a/solution.py
+++ b/solution.py
@@ -8,7 +8,7 @@
 from jax.sharding import PartitionSpec as P
 
 EPSILON = 1e-06
-GROUP = 2
+GROUP = 1
 
 
 def kernel(
@@ -26,14 +26,10 @@
     row = lax.axis_index("rows")
     last = sections - 1
 
-    place = {
-        (1, 0): 0, (1, 2): 1, (2, 0): 2, (2, 2): 3,
-        (1, 1): 4, (2, 1): 5,
-        (0, 0): 6, (0, 2): 7, (0, 1): 8,
-    }
-    own_taps = ((1, 1), (2, 1))
-    halo_taps = ((1, 0), (1, 2), (2, 0), (2, 2))
-    old_taps = ((0, 0), (0, 2), (0, 1))
+    own_taps = ((2, 1),)
+    halo_taps = ((2, 0), (2, 2))
+    old_taps = ((0, 0), (0, 2), (0, 1), (1, 0), (1, 2), (1, 1))
+    place = {tap: at for at, tap in enumerate(own_taps + halo_taps + old_taps)}
 
     def weight_copy(i, j, k):
         return pltpu.make_async_copy(
@@ -162,10 +158,6 @@
     def step(item, carry):
         t0 = item * group
 
-        @pl.when(item > 0)
-        def _():
-            total[...] = product((t0,), 0, 3 * ch, 6)
-
         @pl.when((section > 0) | (item >= per_block))
         def _():
             pass_copy(item).wait_recv()
@@ -188,16 +180,15 @@
         def _():
             weights_here(own_taps)
 
-        own = product((t0 + 1, t0 + 2), 2 * ch, 3 * ch, 4)
+        total[...] = product((t0 + 2,), 2 * ch, 3 * ch, 0)
 
         @pl.when(item == 0)
         def _():
-            total[...] = own
             weights_here(halo_taps)
 
         @pl.when(item > 0)
         def _():
-            total[...] += own
+            total[...] += product((t0, t0 + 1), 0, 3 * ch, 3)
 
         @pl.when(row < row_count - 1)
         def _():
@@ -207,7 +198,7 @@
         def _():
             halo_copy(item, 1).wait_recv()
 
-        summed = total[...] + product((t0 + 1, t0 + 2), 0, 2 * ch, 0)
+        summed = total[...] + product((t0 + 2,), 0, 2 * ch, 1)
         left = pltpu.roll(summed[:, 0:ch], 1, 0)
         left = jnp.where(col_id == 0, 0.0, left)
         right = pltpu.roll(summed[:, 2 * ch : 3 * ch], rows - 1, 0)
@@ -285,7 +276,7 @@
         out = pl.pallas_call(
             functools.partial(kernel, sections, row_count, group),
             out_shape=jax.ShapeDtypeStruct((frames, cols, ch), jnp.bfloat16),
-            in_specs=[pl.BlockSpec(memory_space=pl.ANY)] * 4,
+            in_specs=[pl.BlockSpec(memory_space=pltpu.HBM)] * 4,
             out_specs=vmem,
             scratch_shapes=[
                 pltpu.VMEM((9 * ch, 3 * ch), jnp.bfloat16),
@@ -305,7 +296,7 @@
                 dma((per_block,)),
             ],
             compiler_params=pltpu.CompilerParams(
-                collective_id=0, has_side_effects=True, vmem_limit_bytes=60 * 2**20
+                collective_id=0, has_side_effects=True, vmem_limit_bytes=58 * 2**20
             ),
             cost_estimate=pl.CostEstimate(
                 flops=2 * all_frames * cols * 27 * ch * ch,

time: 48.6 us -> 53.5 us (1.10)
  Pallas kernels: 47 us -> 51.9 us
    pallas_call x1, Pallas kernels: 47 us -> 51.9 us  [body(): pl.pallas_call(functools.partial(kernel, sections, row_count, group), out...]
where the time goes in v3:
time: 53.5 us; the launch traced here: 53.4 us
  Pallas kernels  51.9 us (97%)
  local copies, waits for them, and re-layouts  1.52 us (3%)
    pallas_call x1, Pallas kernels, body(): pl.pallas_call(functools.partial(kernel, sections, row_count, group), out...  51.9 us
    unnamed x1, local copies, waits for them, and re-layouts  1.52 us

profile of v3, /device:TPU:27, one launch (start us, length us, event | category | flops | bytes accessed | tf_op | source)
XLA Modules:
  0.0 53.4 jit_solution(6125232913700812118)
XLA Ops:
  0.0 51.9 %shard_map.46 = bf16[2,48,384]{2,1,0:T(8,128)(2,1)} custom-call(bf16[2,48,384]{2,1,0:T(8,128)(2,1)} %bitcast.7, bf16[3,3,3,384,384]{4,3,2,1,0:T(8,128)(2,1)} %bitcast.6, f32[1,384]{1,0:T(1,128)} %gain_hbm.1, f32[1,384]{1,0:T(1,128)} %bias_hbm.1), custom_call_target="tpu_custom_call" | custom-call | flops 3057647616 | bytes 7962624 | tf_op jit(solution)/shard_map/pallas_call | solution.py:276
  51.9 1.5 %copy.7 = bf16[1,2,1,48,384]{4,3,2,1,0:T(8,128)(2,1)} copy(bf16[1,2,1,48,384]{4,3,2,1,0:T(8,128)(2,1)} %bitcast.5) | data formatting | bytes 147456

commit v4 on v2

--- a/solution.py
+++ b/solution.py
@@ -1,4 +1,5 @@
 import functools
+import math
 
 import jax
 import jax.numpy as jnp
@@ -12,7 +13,7 @@
 
 
 def kernel(
-    sections, row_count, group,
+    sections, row_count, side, group,
     lat_ref, w_hbm, gain_hbm, bias_hbm, o_ref,
     weights, acts, incoming, outgoing, total, gain_ref, bias_ref,
     w_sem, small_sem, lat_send, in_recv, out_send, halo_send, halo_recv, own_recv,
@@ -23,8 +24,38 @@
     items = sections * per_block
     rows = group * cols
     section = lax.axis_index("section")
-    row = lax.axis_index("rows")
+    place_at = lax.axis_index("rows")
     last = sections - 1
+
+    def dealt(index):
+        chip = index // 2
+        line = chip // side
+        along = chip % side
+        turned = along + (line % 2) * (side - 1 - 2 * along)
+        return (line * side + turned) * 2 + index % 2
+
+    row = dealt(place_at)
+    stays = row == place_at
+
+    barrier = pltpu.get_barrier_semaphore()
+    for peer in range(sections):
+        @pl.when(section != peer)
+        def _():
+            pl.semaphore_signal(barrier, inc=1, device_id={"section": peer})
+
+        @pl.when(jnp.logical_not(stays))
+        def _():
+            pl.semaphore_signal(
+                barrier, inc=1, device_id={"section": peer, "rows": row}
+            )
+
+    @pl.when(row > 0)
+    def _():
+        pl.semaphore_signal(barrier, inc=1, device_id={"rows": dealt(row - 1)})
+
+    @pl.when(row < row_count - 1)
+    def _():
+        pl.semaphore_signal(barrier, inc=1, device_id={"rows": dealt(row + 1)})
 
     place = {
         (1, 0): 0, (1, 2): 1, (2, 0): 2, (2, 2): 3,
@@ -53,30 +84,16 @@
         lat_ref, incoming.at[pl.ds(0, frames)], small_sem.at[2]
     )
 
-    @pl.when(section == 0)
+    @pl.when((section == 0) & stays)
     def _():
         first_copy.start()
 
     gain_copy.start()
     bias_copy.start()
-    for i, j in own_taps + halo_taps + old_taps:
+    for i, j in own_taps + halo_taps:
         for k in range(3):
             weight_copy(i, j, k).start()
 
-    barrier = pltpu.get_barrier_semaphore()
-    for peer in range(sections):
-        @pl.when(section != peer)
-        def _():
-            pl.semaphore_signal(barrier, inc=1, device_id={"section": peer})
-
-    @pl.when(row > 0)
-    def _():
-        pl.semaphore_signal(barrier, inc=1, device_id={"rows": row - 1})
-
-    @pl.when(row < row_count - 1)
-    def _():
-        pl.semaphore_signal(barrier, inc=1, device_id={"rows": row + 1})
-
     acts[0:2] = jnp.zeros((2, cols, 3 * ch), jnp.bfloat16)
 
     @pl.when(row == 0)
@@ -88,7 +105,10 @@
         acts[:, :, ch : 2 * ch] = jnp.zeros((all_frames + 2, cols, ch), jnp.bfloat16)
 
     greeted = (
-        sections - 1 + jnp.where(row > 0, 1, 0) + jnp.where(row < row_count - 1, 1, 0)
+        sections - 1
+        + jnp.where(stays, 0, sections)
+        + jnp.where(row > 0, 1, 0)
+        + jnp.where(row < row_count - 1, 1, 0)
     )
     pl.semaphore_wait(barrier, greeted)
 
@@ -98,10 +118,12 @@
             incoming.at[pl.ds(section * frames + part * group, group)],
             lat_send.at[part],
             in_recv.at[section * per_block + part],
-            device_id={"section": 0},
-        )
-
-    @pl.when(section > 0)
+            device_id={"section": 0, "rows": row},
+        )
+
+    sends_in = (section > 0) | jnp.logical_not(stays)
+
+    @pl.when(sends_in)
     def _():
         for part in range(per_block):
             lat_copy(part).start()
@@ -124,18 +146,18 @@
             o_ref.at[pl.ds(part * group, group)],
             out_send.at[item],
             own_recv.at[part],
-            device_id={"section": item // per_block},
-        )
-
-    def halo_copy(item, side):
+            device_id={"section": item // per_block, "rows": row},
+        )
+
+    def halo_copy(item, way):
         t0 = item * group
-        lane = ch if side == 0 else 0
-        target = row - 1 if side == 0 else row + 1
+        lane = ch if way == 0 else 0
+        target = dealt(row - 1 if way == 0 else row + 1)
         return pltpu.make_async_remote_copy(
             acts.at[pl.ds(t0 + 2, group), :, pl.ds(2 * ch, ch)],
             acts.at[pl.ds(t0 + 2, group), :, pl.ds(lane, ch)],
-            halo_send.at[item, side],
-            halo_recv.at[item, side],
+            halo_send.at[item, way],
+            halo_recv.at[item, way],
             device_id={"rows": target},
         )
 
@@ -153,7 +175,7 @@
     gain_row = gain_ref[...]
     bias_row = bias_ref[...]
 
-    @pl.when(section == 0)
+    @pl.when((section == 0) & stays)
     def _():
         first_copy.wait()
 
@@ -162,11 +184,7 @@
     def step(item, carry):
         t0 = item * group
 
-        @pl.when(item > 0)
-        def _():
-            total[...] = product((t0,), 0, 3 * ch, 6)
-
-        @pl.when((section > 0) | (item >= per_block))
+        @pl.when(sends_in | (item >= per_block))
         def _():
             pass_copy(item).wait_recv()
 
@@ -194,10 +212,13 @@
         def _():
             total[...] = own
             weights_here(halo_taps)
+            for i, j in old_taps:
+                for k in range(3):
+                    weight_copy(i, j, k).start()
 
         @pl.when(item > 0)
         def _():
-            total[...] += own
+            total[...] = own + product((t0,), 0, 3 * ch, 6)
 
         @pl.when(row < row_count - 1)
         def _():
@@ -215,7 +236,7 @@
         y = x + (left + summed[:, ch : 2 * ch] + right) + bias_row
         y = y.astype(jnp.bfloat16).reshape(group, cols, ch)
 
-        home = (section == last) & (item >= last * per_block)
+        home = (section == last) & (item >= last * per_block) & stays
 
         @pl.when(home)
         def _():
@@ -229,7 +250,7 @@
         def _():
             pass_copy(item).start()
 
-        @pl.when((section == last) & (item < last * per_block))
+        @pl.when((section == last) & jnp.logical_not(home))
         def _():
             home_copy(item).start()
 
@@ -241,7 +262,7 @@
 
     lax.fori_loop(0, items, step, 0)
 
-    @pl.when(section > 0)
+    @pl.when(sends_in)
     def _():
         for part in range(per_block):
             lat_copy(part).wait_send()
@@ -255,7 +276,7 @@
         def _():
             halo_copy(item, 1).wait_send()
 
-        @pl.when((section < last) | (item < last * per_block))
+        @pl.when((section < last) | (item < last * per_block) | jnp.logical_not(stays))
         def _():
             pass_copy(item).wait_send()
 
@@ -263,7 +284,7 @@
 
     lax.fori_loop(0, items, finish, 0)
 
-    @pl.when(section < last)
+    @pl.when((section < last) | jnp.logical_not(stays))
     def _():
         for part in range(per_block):
             home_copy(part).wait_recv()
@@ -272,6 +293,9 @@
 def solution(mesh):
     sections = mesh.shape["section"]
     row_count = mesh.shape["rows"]
+    side = math.isqrt(row_count // 2)
+    if 2 * side * side != row_count:
+        side = 1
 
     def body(latents, conv_weight, gain, bias):
         _, frames, _, cols, ch = latents.shape
@@ -283,7 +307,7 @@
         dma = pltpu.SemaphoreType.DMA
         vmem = pl.BlockSpec(memory_space=pltpu.VMEM)
         out = pl.pallas_call(
-            functools.partial(kernel, sections, row_count, group),
+            functools.partial(kernel, sections, row_count, side, group),
             out_shape=jax.ShapeDtypeStruct((frames, cols, ch), jnp.bfloat16),
             in_specs=[pl.BlockSpec(memory_space=pl.ANY)] * 4,
             out_specs=vmem,

time: 48.6 us -> 53.9 us (1.11)
  the two profiles are of different devices: /device:TPU:27 before, /device:TPU:28 now
where the time goes in v4:
time: 53.9 us; the launch traced here: 53.7 us
  Pallas kernels  52.2 us (97%)
  local copies, waits for them, and re-layouts  1.52 us (3%)
    pallas_call x1, Pallas kernels, body(): pl.pallas_call(functools.partial(kernel, sections, row_count, side, group...  52.2 us
    unnamed x1, local copies, waits for them, and re-layouts  1.52 us

profile of v4, /device:TPU:28, one launch (start us, length us, event | category | flops | bytes accessed | tf_op | source)
XLA Modules:
  0.0 53.7 jit_solution(15814070784904017182)
XLA Ops:
  0.0 52.2 %shard_map.46 = bf16[2,48,384]{2,1,0:T(8,128)(2,1)} custom-call(bf16[2,48,384]{2,1,0:T(8,128)(2,1)} %bitcast.7, bf16[3,3,3,384,384]{4,3,2,1,0:T(8,128)(2,1)} %bitcast.6, f32[1,384]{1,0:T(1,128)} %gain_hbm.1, f32[1,384]{1,0:T(1,128)} %bias_hbm.1), custom_call_target="tpu_custom_call" | custom-call | flops 3057647616 | bytes 7962624 | tf_op jit(solution)/shard_map/pallas_call | solution.py:309
  52.2 1.5 %copy.7 = bf16[1,2,1,48,384]{4,3,2,1,0:T(8,128)(2,1)} copy(bf16[1,2,1,48,384]{4,3,2,1,0:T(8,128)(2,1)} %bitcast.5) | data formatting | bytes 147456

commit v5 on v2

--- a/solution.py
+++ b/solution.py
@@ -26,6 +26,20 @@
     row = lax.axis_index("rows")
     last = sections - 1
 
+    barrier = pltpu.get_barrier_semaphore()
+    for peer in range(sections):
+        @pl.when(section != peer)
+        def _():
+            pl.semaphore_signal(barrier, inc=1, device_id={"section": peer})
+
+    @pl.when(row > 0)
+    def _():
+        pl.semaphore_signal(barrier, inc=1, device_id={"rows": row - 1})
+
+    @pl.when(row < row_count - 1)
+    def _():
+        pl.semaphore_signal(barrier, inc=1, device_id={"rows": row + 1})
+
     place = {
         (1, 0): 0, (1, 2): 1, (2, 0): 2, (2, 2): 3,
         (1, 1): 4, (2, 1): 5,
@@ -42,6 +56,11 @@
             w_sem.at[i, j, k],
         )
 
+    def weights_start(taps):
+        for i, j in taps:
+            for k in range(3):
+                weight_copy(i, j, k).start(priority=1)
+
     def weights_here(taps):
         for i, j in taps:
             for k in range(3):
@@ -59,23 +78,12 @@
 
     gain_copy.start()
     bias_copy.start()
-    for i, j in own_taps + halo_taps + old_taps:
-        for k in range(3):
-            weight_copy(i, j, k).start()
-
-    barrier = pltpu.get_barrier_semaphore()
-    for peer in range(sections):
-        @pl.when(section != peer)
-        def _():
-            pl.semaphore_signal(barrier, inc=1, device_id={"section": peer})
-
-    @pl.when(row > 0)
-    def _():
-        pl.semaphore_signal(barrier, inc=1, device_id={"rows": row - 1})
-
-    @pl.when(row < row_count - 1)
-    def _():
-        pl.semaphore_signal(barrier, inc=1, device_id={"rows": row + 1})
+    weights_start(own_taps)
+
+    @pl.when(section > 0)
+    def _():
+        weights_start(halo_taps + old_taps)
+
 
     acts[0:2] = jnp.zeros((2, cols, 3 * ch), jnp.bfloat16)
 
@@ -162,10 +170,6 @@
     def step(item, carry):
         t0 = item * group
 
-        @pl.when(item > 0)
-        def _():
-            total[...] = product((t0,), 0, 3 * ch, 6)
-
         @pl.when((section > 0) | (item >= per_block))
         def _():
             pass_copy(item).wait_recv()
@@ -184,9 +188,17 @@
         def _():
             halo_copy(item, 1).start()
 
+        @pl.when((item == 0) & (section == 0))
+        def _():
+            weights_start(halo_taps)
+
         @pl.when(item == 0)
         def _():
             weights_here(own_taps)
+
+        @pl.when(item == 1)
+        def _():
+            weights_here(old_taps)
 
         own = product((t0 + 1, t0 + 2), 2 * ch, 3 * ch, 4)
 
@@ -197,7 +209,7 @@
 
         @pl.when(item > 0)
         def _():
-            total[...] += own
+            total[...] = own + product((t0,), 0, 3 * ch, 6)
 
         @pl.when(row < row_count - 1)
         def _():
@@ -233,9 +245,9 @@
         def _():
             home_copy(item).start()
 
-        @pl.when(item == 0)
-        def _():
-            weights_here(old_taps)
+        @pl.when((item == 0) & (section == 0))
+        def _():
+            weights_start(old_taps)
 
         return carry
 

time: 48.6 us -> 47.4 us (0.975)
  Pallas kernels: 47 us -> 45.7 us
    pallas_call x1, Pallas kernels: 47 us -> 45.7 us  [body(): pl.pallas_call(functools.partial(kernel, sections, row_count, group), out...]
where the time goes in v5:
time: 47.4 us; the launch traced here: 47.2 us
  Pallas kernels  45.7 us (96%)
  local copies, waits for them, and re-layouts  1.52 us (3%)
    pallas_call x1, Pallas kernels, body(): pl.pallas_call(functools.partial(kernel, sections, row_count, group), out...  45.7 us
    unnamed x1, local copies, waits for them, and re-layouts  1.52 us

profile of v5, /device:TPU:27, one launch (start us, length us, event | category | flops | bytes accessed | tf_op | source)
XLA Modules:
  0.0 47.2 jit_solution(17451684415156254874)
XLA Ops:
  0.0 45.7 %shard_map.46 = bf16[2,48,384]{2,1,0:T(8,128)(2,1)} custom-call(bf16[2,48,384]{2,1,0:T(8,128)(2,1)} %bitcast.7, bf16[3,3,3,384,384]{4,3,2,1,0:T(8,128)(2,1)} %bitcast.6, f32[1,384]{1,0:T(1,128)} %gain_hbm.1, f32[1,384]{1,0:T(1,128)} %bias_hbm.1), custom_call_target="tpu_custom_call" | custom-call | flops 3057647616 | bytes 7962624 | tf_op jit(solution)/shard_map/pallas_call | solution.py:297
  45.7 1.5 %copy.7 = bf16[1,2,1,48,384]{4,3,2,1,0:T(8,128)(2,1)} copy(bf16[1,2,1,48,384]{4,3,2,1,0:T(8,128)(2,1)} %bitcast.5) | data formatting | bytes 147456

commit v6 on v5

v6 whole, which is shorter than its diff:
```python
import functools

import jax
import jax.numpy as jnp
from jax import lax
from jax.experimental import pallas as pl
from jax.experimental.pallas import tpu as pltpu
from jax.sharding import PartitionSpec as P

EPSILON = 1e-06
GROUP = 2


def kernel(
    sections, row_count, group,
    lat_ref, w_hbm, gain_hbm, bias_hbm, o_ref,
    weights, acts, incoming, outgoing, total, gain_ref, bias_ref,
    w_sem, small_sem, lat_send, in_recv, out_send, halo_send, halo_recv, own_recv,
):
    frames, cols, ch = lat_ref.shape
    all_frames = sections * frames
    per_block = frames // group
    items = sections * per_block
    rows = group * cols
    section = lax.axis_index("section")
    row = lax.axis_index("rows")
    last = sections - 1

    barrier = pltpu.get_barrier_semaphore()
    for peer in range(sections):
        copies_here = (
            (peer == section - 1)
            | ((section == 0) & (peer > 0))
            | ((peer == last) & (section < last))
        )

        @pl.when(copies_here)
        def _():
            pl.semaphore_signal(barrier, inc=1, device_id={"section": peer})

    @pl.when(row > 0)
    def _():
        pl.semaphore_signal(barrier, inc=1, device_id={"rows": row - 1})

    @pl.when(row < row_count - 1)
    def _():
        pl.semaphore_signal(barrier, inc=1, device_id={"rows": row + 1})

    place = {
        (1, 0): 0, (1, 2): 1, (2, 0): 2, (2, 2): 3,
        (1, 1): 4, (2, 1): 5,
        (0, 0): 6, (0, 2): 7, (0, 1): 8,
    }
    own_taps = ((1, 1), (2, 1))
    halo_taps = ((1, 0), (1, 2), (2, 0), (2, 2))
    old_taps = ((0, 0), (0, 2), (0, 1))

    def weight_copy(i, j, k):
        return pltpu.make_async_copy(
            w_hbm.at[i, j, k],
            weights.at[pl.ds(place[i, j] * ch, ch), pl.ds(k * ch, ch)],
            w_sem.at[i, j, k],
        )

    def weights_start(taps):
        for i, j in taps:
            for k in range(3):
                weight_copy(i, j, k).start(priority=1)

    def weights_here(taps):
        for i, j in taps:
            for k in range(3):
                weight_copy(i, j, k).wait()

    gain_copy = pltpu.make_async_copy(gain_hbm, gain_ref, small_sem.at[0])
    bias_copy = pltpu.make_async_copy(bias_hbm, bias_ref, small_sem.at[1])
    first_copy = pltpu.make_async_copy(
        lat_ref, incoming.at[pl.ds(0, frames)], small_sem.at[2]
    )

    @pl.when(section == 0)
    def _():
        first_copy.start()

    gain_copy.start()
    bias_copy.start()
    weights_start(own_taps)

    @pl.when(section > 0)
    def _():
        weights_start(halo_taps + old_taps)


    acts[:, 0:2] = jnp.zeros((3, 2, cols, ch), jnp.bfloat16)

    @pl.when(row == 0)
    def _():
        acts[0] = jnp.zeros((all_frames + 2, cols, ch), jnp.bfloat16)

    @pl.when(row == row_count - 1)
    def _():
        acts[1] = jnp.zeros((all_frames + 2, cols, ch), jnp.bfloat16)

    greeted = (
        jnp.where(
            section == last, last, jnp.where(section > 0, 2, 1)
        )
        + jnp.where(row > 0, 1, 0)
        + jnp.where(row < row_count - 1, 1, 0)
    )

    def lat_copy(part):
        return pltpu.make_async_remote_copy(
            lat_ref.at[part],
            incoming.at[section * frames + part],
            lat_send.at[part],
            in_recv.at[section * frames + part],
            device_id={"section": 0},
        )

    @pl.when(section > 0)
    def _():
        pl.semaphore_wait(barrier, greeted)
        for part in range(frames):
            lat_copy(part).start()

    def pass_copy(t):
        return pltpu.make_async_remote_copy(
            outgoing.at[t],
            incoming.at[t],
            out_send.at[t],
            in_recv.at[t],
            device_id={"section": lax.rem(section + 1, sections)},
        )

    def home_copy(t):
        part = lax.rem(t, frames)
        return pltpu.make_async_remote_copy(
            outgoing.at[t],
            o_ref.at[part],
            out_send.at[t],
            own_recv.at[part],
            device_id={"section": t // frames},
        )

    def halo_copy(t, way):
        lane = 1 if way == 0 else 0
        target = row - 1 if way == 0 else row + 1
        return pltpu.make_async_remote_copy(
            acts.at[2, t + 2],
            acts.at[lane, t + 2],
            halo_send.at[t, way],
            halo_recv.at[t, way],
            device_id={"rows": target},
        )

    def product(starts, places, top):
        parts = [
            acts[at, pl.ds(start, group)].reshape(rows, ch)
            for start in starts
            for at in places
        ]
        lhs = jnp.concatenate(parts, axis=-1)
        rhs = weights[top * ch : top * ch + lhs.shape[1], :]
        return jnp.dot(lhs, rhs, preferred_element_type=jnp.float32)

    gain_copy.wait()
    bias_copy.wait()
    gain_row = gain_ref[...]
    bias_row = bias_ref[...]

    @pl.when(section == 0)
    def _():
        first_copy.wait()

    col_id = lax.broadcasted_iota(jnp.int32, (cols, ch), 0)

    def step(item, carry):
        t0 = item * group

        for part in range(group):
            t = t0 + part

            @pl.when((section > 0) | (item >= per_block))
            def _():
                pass_copy(t).wait_recv()

            x = incoming[t].astype(jnp.float32)
            mean_square = jnp.mean(x * x, axis=-1, keepdims=True)
            v = x * lax.rsqrt(mean_square + EPSILON) * gain_row
            acts[2, t + 2] = (v * jax.nn.sigmoid(v)).astype(jnp.bfloat16)

            if part == 0:
                @pl.when((section == 0) & (item == 0))
                def _():
                    pl.semaphore_wait(barrier, greeted)

            @pl.when(row > 0)
            def _():
                halo_copy(t, 0).start()

            @pl.when(row < row_count - 1)
            def _():
                halo_copy(t, 1).start()

        @pl.when((item == 0) & (section == 0))
        def _():
            weights_start(halo_taps)

        @pl.when(item == 0)
        def _():
            weights_here(own_taps)

        @pl.when(item == 1)
        def _():
            weights_here(old_taps)

        own = product((t0 + 1, t0 + 2), (2,), 4)

        @pl.when(item == 0)
        def _():
            total[...] = own
            weights_here(halo_taps)

        @pl.when(item > 0)
        def _():
            total[...] = own + product((t0,), (0, 1, 2), 6)

        for part in range(group):
            @pl.when(row < row_count - 1)
            def _():
                halo_copy(t0 + part, 0).wait_recv()

            @pl.when(row > 0)
            def _():
                halo_copy(t0 + part, 1).wait_recv()

        summed = total[...] + product((t0 + 1, t0 + 2), (0, 1), 0)
        home = (section == last) & (item >= last * per_block)
        for part in range(group):
            t = t0 + part
            here = summed[part * cols : (part + 1) * cols]
            left = pltpu.roll(here[:, 0:ch], 1, 0)
            left = jnp.where(col_id == 0, 0.0, left)
            right = pltpu.roll(here[:, 2 * ch : 3 * ch], cols - 1, 0)
            right = jnp.where(col_id == cols - 1, 0.0, right)
            x = incoming[t].astype(jnp.float32)
            y = x + (left + here[:, ch : 2 * ch] + right) + bias_row
            y = y.astype(jnp.bfloat16)

            @pl.when(home)
            def _():
                o_ref[t - last * frames] = y

            @pl.when(jnp.logical_not(home))
            def _():
                outgoing[t] = y

            @pl.when(section < last)
            def _():
                pass_copy(t).start()

            @pl.when((section == last) & (item < last * per_block))
            def _():
                home_copy(t).start()

        @pl.when((item == 0) & (section == 0))
        def _():
            weights_start(old_taps)

        return carry

    lax.fori_loop(0, items, step, 0)

    @pl.when(section > 0)
    def _():
        for part in range(frames):
            lat_copy(part).wait_send()

    def finish(t, carry):
        @pl.when(row > 0)
        def _():
            halo_copy(t, 0).wait_send()

        @pl.when(row < row_count - 1)
        def _():
            halo_copy(t, 1).wait_send()

        @pl.when((section < last) | (t < last * frames))
        def _():
            pass_copy(t).wait_send()

        return carry

    lax.fori_loop(0, all_frames, finish, 0)

    @pl.when(section < last)
    def _():
        for part in range(frames):
            home_copy(part).wait_recv()


def solution(mesh):
    sections = mesh.shape["section"]
    row_count = mesh.shape["rows"]

    def body(latents, conv_weight, gain, bias):
        _, frames, _, cols, ch = latents.shape
        group = GROUP
        all_frames = sections * frames
        rows = group * cols
        dma = pltpu.SemaphoreType.DMA
        vmem = pl.BlockSpec(memory_space=pltpu.VMEM)
        out = pl.pallas_call(
            functools.partial(kernel, sections, row_count, group),
            out_shape=jax.ShapeDtypeStruct((frames, cols, ch), jnp.bfloat16),
            in_specs=[pl.BlockSpec(memory_space=pl.ANY)] * 4,
            out_specs=vmem,
            scratch_shapes=[
                pltpu.VMEM((9 * ch, 3 * ch), jnp.bfloat16),
                pltpu.VMEM((3, all_frames + 2, cols, ch), jnp.bfloat16),
                pltpu.VMEM((all_frames, cols, ch), jnp.bfloat16),
                pltpu.VMEM((all_frames, cols, ch), jnp.bfloat16),
                pltpu.VMEM((rows, 3 * ch), jnp.float32),
                pltpu.VMEM((1, ch), jnp.float32),
                pltpu.VMEM((1, ch), jnp.float32),
                dma((3, 3, 3)),
                dma((3,)),
                dma((frames,)),
                dma((all_frames,)),
                dma((all_frames,)),
                dma((all_frames, 2)),
                dma((all_frames, 2)),
                dma((frames,)),
            ],
            compiler_params=pltpu.CompilerParams(
                collective_id=0, has_side_effects=True, vmem_limit_bytes=60 * 2**20
            ),
            cost_estimate=pl.CostEstimate(
                flops=2 * all_frames * cols * 27 * ch * ch,
                bytes_accessed=27 * ch * ch * 2,
                transcendentals=all_frames * cols * ch,
            ),
        )(latents.reshape(frames, cols, ch), conv_weight[0], gain, bias)
        return out.reshape(latents.shape)

    in_specs = (
        P("section", None, "rows", None, None),
        P("section", None, None, None, None, None),
        P("section", None),
        P("section", None),
    )
    out_specs = P("section", None, "rows", None, None)
    return jax.shard_map(body, mesh=mesh, in_specs=in_specs, out_specs=out_specs, check_vma=False)
```

time: 47.4 us -> 44.4 us (0.937)
  Pallas kernels: 45.7 us -> 42.7 us
    pallas_call x1, Pallas kernels: 45.7 us -> 42.7 us  [body(): pl.pallas_call(functools.partial(kernel, sections, row_count, group), out...]
where the time goes in v6:
time: 44.4 us; the launch traced here: 44.2 us
  Pallas kernels  42.7 us (96%)
  local copies, waits for them, and re-layouts  1.52 us (3%)
    pallas_call x1, Pallas kernels, body(): pl.pallas_call(functools.partial(kernel, sections, row_count, group), out...  42.7 us
    unnamed x1, local copies, waits for them, and re-layouts  1.52 us

profile of v6, /device:TPU:27, one launch (start us, length us, event | category | flops | bytes accessed | tf_op | source)
XLA Modules:
  0.0 44.2 jit_solution(1971765654414632941)
XLA Ops:
  0.0 42.7 %shard_map.46 = bf16[2,48,384]{2,1,0:T(8,128)(2,1)} custom-call(bf16[2,48,384]{2,1,0:T(8,128)(2,1)} %bitcast.7, bf16[3,3,3,384,384]{4,3,2,1,0:T(8,128)(2,1)} %bitcast.6, f32[1,384]{1,0:T(1,128)} %gain_hbm.1, f32[1,384]{1,0:T(1,128)} %bias_hbm.1), custom_call_target="tpu_custom_call" | custom-call | flops 3057647616 | bytes 7962624 | tf_op jit(solution)/shard_map/pallas_call | solution.py:314
  42.7 1.5 %copy.7 = bf16[1,2,1,48,384]{4,3,2,1,0:T(8,128)(2,1)} copy(bf16[1,2,1,48,384]{4,3,2,1,0:T(8,128)(2,1)} %bitcast.5) | data formatting | bytes 147456

commit v7 on v6

--- a/solution.py
+++ b/solution.py
@@ -84,12 +84,7 @@
 
     gain_copy.start()
     bias_copy.start()
-    weights_start(own_taps)
-
-    @pl.when(section > 0)
-    def _():
-        weights_start(halo_taps + old_taps)
-
+    weights_start(own_taps + halo_taps + old_taps)
 
     acts[:, 0:2] = jnp.zeros((3, 2, cols, ch), jnp.bfloat16)
 
@@ -154,14 +149,12 @@
             device_id={"rows": target},
         )
 
-    def product(starts, places, top):
-        parts = [
-            acts[at, pl.ds(start, group)].reshape(rows, ch)
-            for start in starts
-            for at in places
-        ]
-        lhs = jnp.concatenate(parts, axis=-1)
-        rhs = weights[top * ch : top * ch + lhs.shape[1], :]
+    def product(pieces, top):
+        lhs = jnp.concatenate(
+            [acts[at, pl.ds(start, group)].reshape(rows, ch) for at, start in pieces],
+            axis=-1,
+        )
+        rhs = weights[top * ch : (top + len(pieces)) * ch, :]
         return jnp.dot(lhs, rhs, preferred_element_type=jnp.float32)
 
     gain_copy.wait()
@@ -203,28 +196,23 @@
             def _():
                 halo_copy(t, 1).start()
 
-        @pl.when((item == 0) & (section == 0))
-        def _():
-            weights_start(halo_taps)
+        own = ((2, t0 + 1), (2, t0 + 2))
+        old = ((0, t0), (1, t0), (2, t0))
+        halo = ((0, t0 + 1), (1, t0 + 1), (0, t0 + 2), (1, t0 + 2))
 
         @pl.when(item == 0)
         def _():
             weights_here(own_taps)
+            total[...] = product(own, 4)
+            weights_here(halo_taps)
 
         @pl.when(item == 1)
         def _():
             weights_here(old_taps)
 
-        own = product((t0 + 1, t0 + 2), (2,), 4)
-
-        @pl.when(item == 0)
-        def _():
-            total[...] = own
-            weights_here(halo_taps)
-
         @pl.when(item > 0)
         def _():
-            total[...] = own + product((t0,), (0, 1, 2), 6)
+            total[...] = product(own + old, 4)
 
         for part in range(group):
             @pl.when(row < row_count - 1)
@@ -235,7 +223,7 @@
             def _():
                 halo_copy(t0 + part, 1).wait_recv()
 
-        summed = total[...] + product((t0 + 1, t0 + 2), (0, 1), 0)
+        summed = total[...] + product(halo, 0)
         home = (section == last) & (item >= last * per_block)
         for part in range(group):
             t = t0 + part
@@ -263,10 +251,6 @@
             @pl.when((section == last) & (item < last * per_block))
             def _():
                 home_copy(t).start()
-
-        @pl.when((item == 0) & (section == 0))
-        def _():
-            weights_start(old_taps)
 
         return carry
 

time: 44.4 us -> 44.4 us (level)
  no operation moved by 1% of the time
where the time goes in v7:
time: 44.4 us; the launch traced here: 44.3 us
  Pallas kernels  42.8 us (96%)
  local copies, waits for them, and re-layouts  1.52 us (3%)
    pallas_call x1, Pallas kernels, body(): pl.pallas_call(functools.partial(kernel, sections, row_count, group), out...  42.8 us
    unnamed x1, local copies, waits for them, and re-layouts  1.52 us

profile of v7, /device:TPU:27, one launch (start us, length us, event | category | flops | bytes accessed | tf_op | source)
XLA Modules:
  0.0 44.3 jit_solution(10113634625392777074)
XLA Ops:
  0.0 42.8 %shard_map.46 = bf16[2,48,384]{2,1,0:T(8,128)(2,1)} custom-call(bf16[2,48,384]{2,1,0:T(8,128)(2,1)} %bitcast.7, bf16[3,3,3,384,384]{4,3,2,1,0:T(8,128)(2,1)} %bitcast.6, f32[1,384]{1,0:T(1,128)} %gain_hbm.1, f32[1,384]{1,0:T(1,128)} %bias_hbm.1), custom_call_target="tpu_custom_call" | custom-call | flops 3057647616 | bytes 7962624 | tf_op jit(solution)/shard_map/pallas_call | solution.py:298
  42.8 1.5 %copy.7 = bf16[1,2,1,48,384]{4,3,2,1,0:T(8,128)(2,1)} copy(bf16[1,2,1,48,384]{4,3,2,1,0:T(8,128)(2,1)} %bitcast.5) | data formatting | bytes 147456

commit v8 on v7

--- a/solution.py
+++ b/solution.py
@@ -113,6 +113,10 @@
             device_id={"section": 0},
         )
 
+    @pl.when(section >= 2)
+    def _():
+        weights_here(own_taps + halo_taps + old_taps)
+
     @pl.when(section > 0)
     def _():
         pl.semaphore_wait(barrier, greeted)
@@ -149,13 +153,21 @@
             device_id={"rows": target},
         )
 
-    def product(pieces, top):
+    def product(pieces, top, add):
         lhs = jnp.concatenate(
             [acts[at, pl.ds(start, group)].reshape(rows, ch) for at, start in pieces],
             axis=-1,
         )
-        rhs = weights[top * ch : (top + len(pieces)) * ch, :]
-        return jnp.dot(lhs, rhs, preferred_element_type=jnp.float32)
+        for low in range(0, 3 * ch, 256):
+            high = min(low + 256, 3 * ch)
+            part = jnp.dot(
+                lhs,
+                weights[top * ch : (top + len(pieces)) * ch, low:high],
+                preferred_element_type=jnp.float32,
+            )
+            if add:
+                part += total[:, low:high]
+            total[:, low:high] = part
 
     gain_copy.wait()
     bias_copy.wait()
@@ -200,19 +212,25 @@
         old = ((0, t0), (1, t0), (2, t0))
         halo = ((0, t0 + 1), (1, t0 + 1), (0, t0 + 2), (1, t0 + 2))
 
+        @pl.when((item == 0) & (section < 2))
+        def _():
+            weights_here(own_taps)
+
         @pl.when(item == 0)
         def _():
-            weights_here(own_taps)
-            total[...] = product(own, 4)
+            product(own, 4, False)
+
+        @pl.when((item == 0) & (section < 2))
+        def _():
             weights_here(halo_taps)
 
-        @pl.when(item == 1)
+        @pl.when((item == 1) & (section < 2))
         def _():
             weights_here(old_taps)
 
         @pl.when(item > 0)
         def _():
-            total[...] = product(own + old, 4)
+            product(own + old, 4, False)
 
         for part in range(group):
             @pl.when(row < row_count - 1)
@@ -223,11 +241,11 @@
             def _():
                 halo_copy(t0 + part, 1).wait_recv()
 
-        summed = total[...] + product(halo, 0)
+        product(halo, 0, True)
         home = (section == last) & (item >= last * per_block)
         for part in range(group):
             t = t0 + part
-            here = summed[part * cols : (part + 1) * cols]
+            here = total[part * cols : (part + 1) * cols, :]
             left = pltpu.roll(here[:, 0:ch], 1, 0)
             left = jnp.where(col_id == 0, 0.0, left)
             right = pltpu.roll(here[:, 2 * ch : 3 * ch], cols - 1, 0)

time: 44.4 us -> 42.7 us (0.962)
  Pallas kernels: 42.8 us -> 41.1 us
    pallas_call x1, Pallas kernels: 42.8 us -> 41.1 us  [body(): pl.pallas_call(functools.partial(kernel, sections, row_count, group), out...]
where the time goes in v8:
time: 42.7 us; the launch traced here: 42.6 us
  Pallas kernels  41.1 us (96%)
  local copies, waits for them, and re-layouts  1.52 us (4%)
    pallas_call x1, Pallas kernels, body(): pl.pallas_call(functools.partial(kernel, sections, row_count, group), out...  41.1 us
    unnamed x1, local copies, waits for them, and re-layouts  1.52 us

profile of v8, /device:TPU:27, one launch (start us, length us, event | category | flops | bytes accessed | tf_op | source)
XLA Modules:
  0.0 42.6 jit_solution(2739629800448913183)
XLA Ops:
  0.0 41.1 %shard_map.46 = bf16[2,48,384]{2,1,0:T(8,128)(2,1)} custom-call(bf16[2,48,384]{2,1,0:T(8,128)(2,1)} %bitcast.7, bf16[3,3,3,384,384]{4,3,2,1,0:T(8,128)(2,1)} %bitcast.6, f32[1,384]{1,0:T(1,128)} %gain_hbm.1, f32[1,384]{1,0:T(1,128)} %bias_hbm.1), custom_call_target="tpu_custom_call" | custom-call | flops 3057647616 | bytes 7962624 | tf_op jit(solution)/shard_map/pallas_call | solution.py:316
  41.1 1.5 %copy.7 = bf16[1,2,1,48,384]{4,3,2,1,0:T(8,128)(2,1)} copy(bf16[1,2,1,48,384]{4,3,2,1,0:T(8,128)(2,1)} %bitcast.5) | data formatting | bytes 147456

commit v9 on v8

--- a/solution.py
+++ b/solution.py
@@ -200,11 +200,15 @@
                 def _():
                     pl.semaphore_wait(barrier, greeted)
 
+            @pl.when((row % 2 == 1) & (row < row_count - 1))
+            def _():
+                halo_copy(t, 1).start()
+
             @pl.when(row > 0)
             def _():
                 halo_copy(t, 0).start()
 
-            @pl.when(row < row_count - 1)
+            @pl.when((row % 2 == 0) & (row < row_count - 1))
             def _():
                 halo_copy(t, 1).start()
 
@@ -241,7 +245,11 @@
             def _():
                 halo_copy(t0 + part, 1).wait_recv()
 
-        product(halo, 0, True)
+            if part == 0:
+                product(halo[:2], 0, True)
+            if part == group - 1:
+                product(halo[2:], 2, True)
+
         home = (section == last) & (item >= last * per_block)
         for part in range(group):
             t = t0 + part

time: 42.7 us -> 41.4 us (0.970)
  Pallas kernels: 41.1 us -> 39.7 us
    pallas_call x1, Pallas kernels: 41.1 us -> 39.7 us  [body(): pl.pallas_call(functools.partial(kernel, sections, row_count, group), out...]
where the time goes in v9:
time: 41.4 us; the launch traced here: 41.3 us
  Pallas kernels  39.7 us (96%)
  local copies, waits for them, and re-layouts  1.52 us (4%)
    pallas_call x1, Pallas kernels, body(): pl.pallas_call(functools.partial(kernel, sections, row_count, group), out...  39.7 us
    unnamed x1, local copies, waits for them, and re-layouts  1.52 us

profile of v9, /device:TPU:27, one launch (start us, length us, event | category | flops | bytes accessed | tf_op | source)
XLA Modules:
  0.0 41.3 jit_solution(17218051186308855122)
XLA Ops:
  0.0 39.7 %shard_map.46 = bf16[2,48,384]{2,1,0:T(8,128)(2,1)} custom-call(bf16[2,48,384]{2,1,0:T(8,128)(2,1)} %bitcast.7, bf16[3,3,3,384,384]{4,3,2,1,0:T(8,128)(2,1)} %bitcast.6, f32[1,384]{1,0:T(1,128)} %gain_hbm.1, f32[1,384]{1,0:T(1,128)} %bias_hbm.1), custom_call_target="tpu_custom_call" | custom-call | flops 3057647616 | bytes 7962624 | tf_op jit(solution)/shard_map/pallas_call | solution.py:324
  39.8 1.5 %copy.7 = bf16[1,2,1,48,384]{4,3,2,1,0:T(8,128)(2,1)} copy(bf16[1,2,1,48,384]{4,3,2,1,0:T(8,128)(2,1)} %bitcast.5) | data formatting | bytes 147456

commit v10 on v9

--- a/solution.py
+++ b/solution.py
@@ -180,9 +180,8 @@
 
     col_id = lax.broadcasted_iota(jnp.int32, (cols, ch), 0)
 
-    def step(item, carry):
+    def activate(item):
         t0 = item * group
-
         for part in range(group):
             t = t0 + part
 
@@ -212,6 +211,11 @@
             def _():
                 halo_copy(t, 1).start()
 
+    activate(jnp.int32(0))
+
+    def step(item, carry):
+        t0 = item * group
+
         own = ((2, t0 + 1), (2, t0 + 2))
         old = ((0, t0), (1, t0), (2, t0))
         halo = ((0, t0 + 1), (1, t0 + 1), (0, t0 + 2), (1, t0 + 2))
@@ -235,6 +239,10 @@
         @pl.when(item > 0)
         def _():
             product(own + old, 4, False)
+
+        @pl.when((item > 0) & (item < items - 1))
+        def _():
+            activate(item + 1)
 
         for part in range(group):
             @pl.when(row < row_count - 1)
@@ -277,6 +285,10 @@
             @pl.when((section == last) & (item < last * per_block))
             def _():
                 home_copy(t).start()
+
+        @pl.when((item == 0) & (items > 1))
+        def _():
+            activate(item + 1)
 
         return carry
 

time: 41.4 us -> 41 us (level)
  the two profiles are of different devices: /device:TPU:27 before, /device:TPU:20 now
where the time goes in v10:
time: 41 us; the launch traced here: 40.8 us
  Pallas kernels  39.3 us (96%)
  local copies, waits for them, and re-layouts  1.52 us (4%)
    pallas_call x1, Pallas kernels, body(): pl.pallas_call(functools.partial(kernel, sections, row_count, group), out...  39.3 us
    unnamed x1, local copies, waits for them, and re-layouts  1.52 us

profile of v10, /device:TPU:20, one launch (start us, length us, event | category | flops | bytes accessed | tf_op | source)
XLA Modules:
  0.0 40.8 jit_solution(1521744135732934755)
XLA Ops:
  0.0 39.3 %shard_map.46 = bf16[2,48,384]{2,1,0:T(8,128)(2,1)} custom-call(bf16[2,48,384]{2,1,0:T(8,128)(2,1)} %bitcast.7, bf16[3,3,3,384,384]{4,3,2,1,0:T(8,128)(2,1)} %bitcast.6, f32[1,384]{1,0:T(1,128)} %gain_hbm.1, f32[1,384]{1,0:T(1,128)} %bias_hbm.1), custom_call_target="tpu_custom_call" | custom-call | flops 3057647616 | bytes 7962624 | tf_op jit(solution)/shard_map/pallas_call | solution.py:336
  39.3 1.5 %copy.7 = bf16[1,2,1,48,384]{4,3,2,1,0:T(8,128)(2,1)} copy(bf16[1,2,1,48,384]{4,3,2,1,0:T(8,128)(2,1)} %bitcast.5) | data formatting | bytes 147456

commit v11 on v10

--- a/solution.py
+++ b/solution.py
@@ -213,6 +213,21 @@
 
     activate(jnp.int32(0))
 
+    def finish(t, carry):
+        @pl.when(row > 0)
+        def _():
+            halo_copy(t, 0).wait_send()
+
+        @pl.when(row < row_count - 1)
+        def _():
+            halo_copy(t, 1).wait_send()
+
+        @pl.when((section < last) | (t < last * frames))
+        def _():
+            pass_copy(t).wait_send()
+
+        return carry
+
     def step(item, carry):
         t0 = item * group
 
@@ -243,6 +258,11 @@
         @pl.when((item > 0) & (item < items - 1))
         def _():
             activate(item + 1)
+
+        @pl.when(item > 0)
+        def _():
+            for part in range(group):
+                finish(t0 - group + part, 0)
 
         for part in range(group):
             @pl.when(row < row_count - 1)
@@ -299,22 +319,7 @@
         for part in range(frames):
             lat_copy(part).wait_send()
 
-    def finish(t, carry):
-        @pl.when(row > 0)
-        def _():
-            halo_copy(t, 0).wait_send()
-
-        @pl.when(row < row_count - 1)
-        def _():
-            halo_copy(t, 1).wait_send()
-
-        @pl.when((section < last) | (t < last * frames))
-        def _():
-            pass_copy(t).wait_send()
-
-        return carry
-
-    lax.fori_loop(0, all_frames, finish, 0)
+    lax.fori_loop(all_frames - group, all_frames, finish, 0)
 
     @pl.when(section < last)
     def _():

time: 41 us -> 44.6 us (1.088)
  the two profiles are of different devices: /device:TPU:20 before, /device:TPU:22 now
where the time goes in v11:
time: 44.6 us; the launch traced here: 44.4 us
  Pallas kernels  42.9 us (96%)
  local copies, waits for them, and re-layouts  1.52 us (3%)
    pallas_call x1, Pallas kernels, body(): pl.pallas_call(functools.partial(kernel, sections, row_count, group), out...  42.9 us
    unnamed x1, local copies, waits for them, and re-layouts  1.52 us

profile of v11, /device:TPU:22, one launch (start us, length us, event | category | flops | bytes accessed | tf_op | source)
XLA Modules:
  0.0 44.4 jit_solution(17577093416280662918)
XLA Ops:
  0.0 42.9 %shard_map.46 = bf16[2,48,384]{2,1,0:T(8,128)(2,1)} custom-call(bf16[2,48,384]{2,1,0:T(8,128)(2,1)} %bitcast.7, bf16[3,3,3,384,384]{4,3,2,1,0:T(8,128)(2,1)} %bitcast.6, f32[1,384]{1,0:T(1,128)} %gain_hbm.1, f32[1,384]{1,0:T(1,128)} %bias_hbm.1), custom_call_target="tpu_custom_call" | custom-call | flops 3057647616 | bytes 7962624 | tf_op jit(solution)/shard_map/pallas_call | solution.py:341
  42.9 1.5 %copy.7 = bf16[1,2,1,48,384]{4,3,2,1,0:T(8,128)(2,1)} copy(bf16[1,2,1,48,384]{4,3,2,1,0:T(8,128)(2,1)} %bitcast.5) | data formatting | bytes 147456
